TPU v7x, 256 devices: a whole 4x4x8 slice. The times are simulated.
256 devices in a mesh: dp: 2 (over y_lo), ctx: 16 (over x, y_hi, core), tp: 8 (over z).
Axes of the slice: x: 4, y: 4 (y_hi: 2, y_lo: 2; y = y_hi * 2 + y_lo), z: 8, core: 2. Of those that a mesh axis runs over, the one named last changes fastest.
Arguments:
- q_prompt: bfloat16 [4, 3072, 16384], P('dp', 'ctx', 'tp'), parts along dimension 0, may hold values from -8 to 8
- k_prompt: bfloat16 [4, 3072, 1024], P('dp', 'ctx', 'tp'), parts along dimension 0, may hold values from -8 to 8
- v_prompt: bfloat16 [4, 3072, 1024], P('dp', 'ctx', 'tp'), parts along dimension 0, may hold values from -6 to 6
- q_follow: bfloat16 [4, 512, 16384], P('dp', 'ctx', 'tp'), parts along dimension 0, may hold values from -8 to 8
- k_follow: bfloat16 [4, 512, 1024], P('dp', 'ctx', 'tp'), parts along dimension 0, may hold values from -8 to 8
- v_follow: bfloat16 [4, 512, 1024], P('dp', 'ctx', 'tp'), parts along dimension 0, may hold values from -6 to 6
- lengths: int32 [4, 2], P('dp'), parts along dimension 0, may hold values from 256 to 3072, as said below
- block_order: int32 [4, 32], P('dp'), parts along dimension 0, may hold values from 0 to 31, as said below
Outputs:
- attn_prompt: bfloat16 [4, 3072, 16384], P('dp', 'ctx', 'tp'), parts along dimension 0
- attn_follow: bfloat16 [4, 512, 16384], P('dp', 'ctx', 'tp'), parts along dimension 0
There are 2 independent parts, one for each index of `dp`. A program takes and returns all parts, laid end to end along the dimension named above; each array names one. Nothing has to cross between parts.
Inputs may be any that keep to these rules, and one draw needn't show every extreme that they name: In each part, one conversation drawn from the seed has lengths exactly 3072 and 512; every prompt length lies in 1536 to 3072, every follow-up length in 256 to 512. `block_order`: for each conversation, block slots 2 d and 2 d + 1 hold blocks b and 31 - b; every block appears once.
All inputs are finite; a program needn't handle non-finite values.
Results may differ from a plain program's by a relative error of at most 0.033.
Values may be sent and summed in bfloat16 or wider, within the bound.
A program may use at most 64 MiB of HBM per device.

v0:
```python
import math

import jax
import jax.numpy as jnp
from jax import lax
from jax.sharding import PartitionSpec as P

HEAD_DIM = 128


def slot_positions(order_row, slot_ids, block_rows):
    onehot = (
        slot_ids[:, None] // block_rows == jnp.arange(order_row.shape[0], dtype=jnp.int32)[None, :]
    )
    picked = jnp.sum(jnp.where(onehot, order_row[None, :], 0), axis=1)
    return picked * block_rows + slot_ids % block_rows


def split_heads(query, key_width):
    row_count = query.shape[0]
    key_heads = key_width // HEAD_DIM
    group_size = query.shape[1] // key_width
    return query.reshape(row_count, key_heads, group_size, HEAD_DIM).transpose(1, 2, 0, 3)


def absorb(carried, query4, key_rows, value_rows, query_key, key_key, key_live):
    running_max, weight_sum, accumulated = carried
    keys3 = key_rows.reshape(key_rows.shape[0], -1, HEAD_DIM)
    values3 = value_rows.reshape(value_rows.shape[0], -1, HEAD_DIM)
    scores = jnp.einsum("hgrd,khd->hgrk", query4, keys3, preferred_element_type=jnp.float32) * (
        1.0 / math.sqrt(HEAD_DIM)
    )
    visible = (key_key[None, :] <= query_key[:, None]) & key_live[None, :]
    scores = jnp.where(visible, scores, jnp.float32(-1e30))
    new_max = jnp.maximum(running_max, jnp.max(scores, axis=-1))
    weights = jnp.where(visible, jnp.exp(scores - new_max[..., None]), jnp.float32(0.0))
    factor = jnp.exp(running_max - new_max)
    weight_sum = weight_sum * factor + jnp.sum(weights, axis=-1)
    product = jnp.einsum(
        "hgrk,khd->hgrd", weights.astype(jnp.bfloat16), values3, preferred_element_type=jnp.float32
    )
    accumulated = accumulated * factor[..., None] + product
    return (new_max, weight_sum, accumulated)


def absorb_blocked(carried, query4, key_rows, value_rows, query_key, key_key, key_live):
    total_rows = key_rows.shape[0]
    pieces = total_rows // 512

    def scan_step(inner, operands):
        return (
            absorb(inner, query4, operands[0], operands[1], query_key, operands[2], operands[3]),
            None,
        )

    operands = (
        key_rows.reshape(pieces, 512, key_rows.shape[1]),
        value_rows.reshape(pieces, 512, value_rows.shape[1]),
        key_key.reshape(pieces, 512),
        key_live.reshape(pieces, 512),
    )
    carried, unused = lax.scan(scan_step, carried, operands)
    return carried


def empty_state(conv_count, key_heads, group_size, row_count):
    running_max = jnp.full((conv_count, key_heads, group_size, row_count), -1e30, jnp.float32)
    weight_sum = jnp.zeros((conv_count, key_heads, group_size, row_count), jnp.float32)
    accumulated = jnp.zeros((conv_count, key_heads, group_size, row_count, HEAD_DIM), jnp.float32)
    return (running_max, weight_sum, accumulated)


def stack_states(results):
    return tuple((jnp.stack([item[m] for item in results]) for m in range(3)))


def finish(carried, live_rows):
    running_max, weight_sum, accumulated = carried
    results = []
    for c in range(accumulated.shape[0]):
        normed = accumulated[c] / weight_sum[c][..., None]
        row_count = normed.shape[2]
        flat = normed.transpose(2, 0, 1, 3).reshape(row_count, -1)
        results.append(
            jnp.where(live_rows[c][:, None], flat, jnp.float32(0.0)).astype(jnp.bfloat16)
        )
    return jnp.stack(results)


def on_device(q_prompt, k_prompt, v_prompt, q_follow, k_follow, v_follow, lengths, block_order):
    cycle_index = lax.axis_index("ctx")
    conv_count, prompt_rows, query_width = q_prompt.shape
    key_width = k_prompt.shape[2]
    follow_rows = q_follow.shape[1]
    block_rows = prompt_rows // 2
    key_heads = key_width // HEAD_DIM
    group_size = query_width // key_width
    own_slots = cycle_index * prompt_rows + jnp.arange(prompt_rows, dtype=jnp.int32)
    own_positions = [
        slot_positions(block_order[c], own_slots, block_rows) for c in range(conv_count)
    ]
    prompt_queries = [split_heads(q_prompt[c], key_width) for c in range(conv_count)]
    follow_ids = cycle_index * follow_rows + jnp.arange(follow_rows, dtype=jnp.int32)
    follow_queries = [split_heads(q_follow[c], key_width) for c in range(conv_count)]
    prompt_start = empty_state(conv_count, key_heads, group_size, prompt_rows)
    follow_start = empty_state(conv_count, key_heads, group_size, follow_rows)
    key_rows = lax.all_gather(k_prompt, "ctx", axis=1, tiled=True)
    value_rows = lax.all_gather(v_prompt, "ctx", axis=1, tiled=True)
    slot_ids = jnp.arange(key_rows.shape[1], dtype=jnp.int32)
    results = []
    for prompt_c in range(conv_count):
        key_positions = slot_positions(block_order[prompt_c], slot_ids, block_rows)
        key_live = key_positions < lengths[prompt_c, 0]
        results.append(
            absorb_blocked(
                (prompt_start[0][prompt_c], prompt_start[1][prompt_c], prompt_start[2][prompt_c]),
                prompt_queries[prompt_c],
                key_rows[prompt_c],
                value_rows[prompt_c],
                own_positions[prompt_c],
                key_positions,
                key_live,
            )
        )
    prompt_state = stack_states(results)
    joined_keys = jnp.concatenate([k_prompt, k_follow], axis=1)
    joined_values = jnp.concatenate([v_prompt, v_follow], axis=1)
    stride = prompt_rows + follow_rows
    key_rows = lax.all_gather(joined_keys, "ctx", axis=1, tiled=True)
    value_rows = lax.all_gather(joined_values, "ctx", axis=1, tiled=True)
    row_ids = jnp.arange(key_rows.shape[1], dtype=jnp.int32)
    owner_dev = row_ids // stride
    local_row = row_ids % stride
    is_prompt = local_row < prompt_rows
    slot_ids = owner_dev * prompt_rows + jnp.minimum(local_row, prompt_rows - 1)
    later_ids = owner_dev * follow_rows + local_row - prompt_rows
    key_key = jnp.where(is_prompt, -1, later_ids)
    results = []
    for follow_c in range(conv_count):
        key_positions = slot_positions(block_order[follow_c], slot_ids, block_rows)
        key_live = jnp.where(
            is_prompt, key_positions < lengths[follow_c, 0], later_ids < lengths[follow_c, 1]
        )
        results.append(
            absorb_blocked(
                (follow_start[0][follow_c], follow_start[1][follow_c], follow_start[2][follow_c]),
                follow_queries[follow_c],
                key_rows[follow_c],
                value_rows[follow_c],
                follow_ids,
                key_key,
                key_live,
            )
        )
    follow_state = stack_states(results)
    attn_prompt = finish(
        prompt_state, [own_positions[c] < lengths[c, 0] for c in range(conv_count)]
    )
    attn_follow = finish(follow_state, [follow_ids < lengths[c, 1] for c in range(conv_count)])
    return (attn_prompt, attn_follow)


def solution(mesh):
    return jax.shard_map(
        on_device,
        mesh=mesh,
        in_specs=(
            P("dp", "ctx", "tp"),
            P("dp", "ctx", "tp"),
            P("dp", "ctx", "tp"),
            P("dp", "ctx", "tp"),
            P("dp", "ctx", "tp"),
            P("dp", "ctx", "tp"),
            P("dp", None),
            P("dp", None),
        ),
        out_specs=(P("dp", "ctx", "tp"), P("dp", "ctx", "tp")),
        check_vma=False,
    )
```

profile of v0, /device:TPU:1, one launch (start us, length us, event | category | flops | bytes accessed | tf_op | source)
XLA Modules:
  0.0 326.3 jit_solution(17777257999721808344)
XLA Ops:
  8.7 1.6 pad_maximum_fusion.2
  10.3 1.6 pad_maximum_fusion.3
  12.9 1.5 fusion.117
  15.4 1.5 slice_bitcast_fusion.1
  18.7 1.3 fusion.103
  21.3 1.3 fusion.102
  22.7 1.3 broadcast_compare_fusion.2
  24.0 42.8 %all-gather.5.cloned.1.call-done = bf16[2,3072,128]{2,1,0:T(8,128)(2,1)} async-done(((bf16[2,192,128]{2,1,0:T(8,128)(2,1)}), bf16[2,3072,128]{2,1,0:T(8,128)(2,1)}) %all-gather.5.cloned.1.call-update) | async-done | bytes 1572880 | tf_op jit(solution)/shard_map/all_gather | solution.py:107
  66.8 2.4 fusion.116
  69.2 51.1 %all-gather.7.cloned.1.call-done = bf16[2,3072,128]{2,1,0:T(8,128)(2,1)} async-done(((bf16[2,192,128]{2,1,0:T(8,128)(2,1)}), bf16[2,3072,128]{2,1,0:T(8,128)(2,1)}) %all-gather.7.cloned.1.call-update) | async-done | bytes 1572880 | tf_op jit(solution)/shard_map/all_gather | solution.py:108
  120.3 2.7 fusion.115
  123.0 75.8 %while.60 = (s32[]{:T(128)}, f32[1,16,192]{2,1,0:T(8,128)S(1)}, f32[1,16,192]{2,1,0:T(8,128)S(1)}, f32[1,16,192,128]{3,2,1,0:T(8,128)}, s32[6,512]{1,0:T(8,128)S...) while((s32[]{:T(128)}, f32[1,16,192]{2,1,0:T(8,128)S(1)}, ...), condition=%wide.region_5.6_spmd.clone, body=%wide.region_2.5_spmd.clone.sunk | while | flops 827148288 | bytes 48833952 | solution.py:62
  123.2 4.7 %fusion.142 = (f32[16,192]{1,0:T(8,128)S(1)}, f32[512,16,192]{0,2,1:T(8,128)}) fusion(pred[192,512]{1,0:T(8,128)(4,1)S(1)} %compare_and_fusion.8, bf16[1,16,192,128]{3,2,1,0:T(8,128)(2,1)S(1)} %get-tuple-element.916, bf16[6,512,128]{2,1,0:T(8,128)(2,1)} %get-tuple-element.915, s32[]{:T(128)} %get-tuple-element.896), kind=kOutput, calls=%fused_computation.4.clone.1 | convolution fusion | flops 407368704 | bytes 7320064 | tf_op jit(solution)/shard_map/while/body/eval_jaxpr/hgrd,khd->hgrk/dot_general | solution.py:30
  127.9 5.5 %bitcast_add_fusion.13 = f32[1,16,192,128]{3,2,1,0:T(8,128)} fusion(f32[1,16,192,128]{3,2,1,0:T(8,128)} %get-tuple-element.899, f32[512,16,192]{0,2,1:T(8,128)} %get-tuple-element.804, f32[16,192]{1,0:T(8,128)S(1)} %bitcast.294, pred[192,512]{1,0:T(8,128)(4,1)S(1)} %compare_and_fusion.8, f32[16,192]{1,0:T(8,128)S(1)} %get-tuple-element.805, ...), kind=kOutput, calls=%fused_computation.9.clone.1 | convolution fusion | flops 411697152 | bytes 9691649 | tf_op jit(solution)/shard_map/while/body/eval_jaxpr/hgrk,khd->hgrd/dot_general | solution.py:39
  133.4 2.1 fusion.144
  135.7 4.7 %fusion.142 = (f32[16,192]{1,0:T(8,128)S(1)}, f32[512,16,192]{0,2,1:T(8,128)}) fusion(pred[192,512]{1,0:T(8,128)(4,1)S(1)} %compare_and_fusion.8, bf16[1,16,192,128]{3,2,1,0:T(8,128)(2,1)S(1)} %get-tuple-element.916, bf16[6,512,128]{2,1,0:T(8,128)(2,1)} %get-tuple-element.915, s32[]{:T(128)} %get-tuple-element.896), kind=kOutput, calls=%fused_computation.4.clone.1 | convolution fusion | flops 407368704 | bytes 7320064 | tf_op jit(solution)/shard_map/while/body/eval_jaxpr/hgrd,khd->hgrk/dot_general | solution.py:30
  140.3 5.7 %bitcast_add_fusion.13 = f32[1,16,192,128]{3,2,1,0:T(8,128)} fusion(f32[1,16,192,128]{3,2,1,0:T(8,128)} %get-tuple-element.899, f32[512,16,192]{0,2,1:T(8,128)} %get-tuple-element.804, f32[16,192]{1,0:T(8,128)S(1)} %bitcast.294, pred[192,512]{1,0:T(8,128)(4,1)S(1)} %compare_and_fusion.8, f32[16,192]{1,0:T(8,128)S(1)} %get-tuple-element.805, ...), kind=kOutput, calls=%fused_computation.9.clone.1 | convolution fusion | flops 411697152 | bytes 9691649 | tf_op jit(solution)/shard_map/while/body/eval_jaxpr/hgrk,khd->hgrd/dot_general | solution.py:39
  146.0 2.1 fusion.144
  148.3 4.7 %fusion.142 = (f32[16,192]{1,0:T(8,128)S(1)}, f32[512,16,192]{0,2,1:T(8,128)}) fusion(pred[192,512]{1,0:T(8,128)(4,1)S(1)} %compare_and_fusion.8, bf16[1,16,192,128]{3,2,1,0:T(8,128)(2,1)S(1)} %get-tuple-element.916, bf16[6,512,128]{2,1,0:T(8,128)(2,1)} %get-tuple-element.915, s32[]{:T(128)} %get-tuple-element.896), kind=kOutput, calls=%fused_computation.4.clone.1 | convolution fusion | flops 407368704 | bytes 7320064 | tf_op jit(solution)/shard_map/while/body/eval_jaxpr/hgrd,khd->hgrk/dot_general | solution.py:30
  153.0 5.7 %bitcast_add_fusion.13 = f32[1,16,192,128]{3,2,1,0:T(8,128)} fusion(f32[1,16,192,128]{3,2,1,0:T(8,128)} %get-tuple-element.899, f32[512,16,192]{0,2,1:T(8,128)} %get-tuple-element.804, f32[16,192]{1,0:T(8,128)S(1)} %bitcast.294, pred[192,512]{1,0:T(8,128)(4,1)S(1)} %compare_and_fusion.8, f32[16,192]{1,0:T(8,128)S(1)} %get-tuple-element.805, ...), kind=kOutput, calls=%fused_computation.9.clone.1 | convolution fusion | flops 411697152 | bytes 9691649 | tf_op jit(solution)/shard_map/while/body/eval_jaxpr/hgrk,khd->hgrd/dot_general | solution.py:39
  158.7 2.1 fusion.144
  161.0 4.7 %fusion.142 = (f32[16,192]{1,0:T(8,128)S(1)}, f32[512,16,192]{0,2,1:T(8,128)}) fusion(pred[192,512]{1,0:T(8,128)(4,1)S(1)} %compare_and_fusion.8, bf16[1,16,192,128]{3,2,1,0:T(8,128)(2,1)S(1)} %get-tuple-element.916, bf16[6,512,128]{2,1,0:T(8,128)(2,1)} %get-tuple-element.915, s32[]{:T(128)} %get-tuple-element.896), kind=kOutput, calls=%fused_computation.4.clone.1 | convolution fusion | flops 407368704 | bytes 7320064 | tf_op jit(solution)/shard_map/while/body/eval_jaxpr/hgrd,khd->hgrk/dot_general | solution.py:30
  165.6 5.7 %bitcast_add_fusion.13 = f32[1,16,192,128]{3,2,1,0:T(8,128)} fusion(f32[1,16,192,128]{3,2,1,0:T(8,128)} %get-tuple-element.899, f32[512,16,192]{0,2,1:T(8,128)} %get-tuple-element.804, f32[16,192]{1,0:T(8,128)S(1)} %bitcast.294, pred[192,512]{1,0:T(8,128)(4,1)S(1)} %compare_and_fusion.8, f32[16,192]{1,0:T(8,128)S(1)} %get-tuple-element.805, ...), kind=kOutput, calls=%fused_computation.9.clone.1 | convolution fusion | flops 411697152 | bytes 9691649 | tf_op jit(solution)/shard_map/while/body/eval_jaxpr/hgrk,khd->hgrd/dot_general | solution.py:39
  171.4 2.1 fusion.144
  173.7 4.7 %fusion.142 = (f32[16,192]{1,0:T(8,128)S(1)}, f32[512,16,192]{0,2,1:T(8,128)}) fusion(pred[192,512]{1,0:T(8,128)(4,1)S(1)} %compare_and_fusion.8, bf16[1,16,192,128]{3,2,1,0:T(8,128)(2,1)S(1)} %get-tuple-element.916, bf16[6,512,128]{2,1,0:T(8,128)(2,1)} %get-tuple-element.915, s32[]{:T(128)} %get-tuple-element.896), kind=kOutput, calls=%fused_computation.4.clone.1 | convolution fusion | flops 407368704 | bytes 7320064 | tf_op jit(solution)/shard_map/while/body/eval_jaxpr/hgrd,khd->hgrk/dot_general | solution.py:30
  178.3 5.7 %bitcast_add_fusion.13 = f32[1,16,192,128]{3,2,1,0:T(8,128)} fusion(f32[1,16,192,128]{3,2,1,0:T(8,128)} %get-tuple-element.899, f32[512,16,192]{0,2,1:T(8,128)} %get-tuple-element.804, f32[16,192]{1,0:T(8,128)S(1)} %bitcast.294, pred[192,512]{1,0:T(8,128)(4,1)S(1)} %compare_and_fusion.8, f32[16,192]{1,0:T(8,128)S(1)} %get-tuple-element.805, ...), kind=kOutput, calls=%fused_computation.9.clone.1 | convolution fusion | flops 411697152 | bytes 9691649 | tf_op jit(solution)/shard_map/while/body/eval_jaxpr/hgrk,khd->hgrd/dot_general | solution.py:39
  184.0 2.1 fusion.144
  186.3 4.7 %fusion.142 = (f32[16,192]{1,0:T(8,128)S(1)}, f32[512,16,192]{0,2,1:T(8,128)}) fusion(pred[192,512]{1,0:T(8,128)(4,1)S(1)} %compare_and_fusion.8, bf16[1,16,192,128]{3,2,1,0:T(8,128)(2,1)S(1)} %get-tuple-element.916, bf16[6,512,128]{2,1,0:T(8,128)(2,1)} %get-tuple-element.915, s32[]{:T(128)} %get-tuple-element.896), kind=kOutput, calls=%fused_computation.4.clone.1 | convolution fusion | flops 407368704 | bytes 7320064 | tf_op jit(solution)/shard_map/while/body/eval_jaxpr/hgrd,khd->hgrk/dot_general | solution.py:30
  191.0 5.7 %bitcast_add_fusion.13 = f32[1,16,192,128]{3,2,1,0:T(8,128)} fusion(f32[1,16,192,128]{3,2,1,0:T(8,128)} %get-tuple-element.899, f32[512,16,192]{0,2,1:T(8,128)} %get-tuple-element.804, f32[16,192]{1,0:T(8,128)S(1)} %bitcast.294, pred[192,512]{1,0:T(8,128)(4,1)S(1)} %compare_and_fusion.8, f32[16,192]{1,0:T(8,128)S(1)} %get-tuple-element.805, ...), kind=kOutput, calls=%fused_computation.9.clone.1 | convolution fusion | flops 411697152 | bytes 9691649 | tf_op jit(solution)/shard_map/while/body/eval_jaxpr/hgrk,khd->hgrd/dot_general | solution.py:39
  196.7 2.1 fusion.144
  198.8 69.9 %while.61 = (s32[]{:T(128)}, f32[1,16,192]{2,1,0:T(8,128)S(1)}, f32[1,16,192]{2,1,0:T(8,128)S(1)}, f32[1,16,192,128]{3,2,1,0:T(8,128)}, s32[6,512]{1,0:T(8,128)S...) while((s32[]{:T(128)}, f32[1,16,192]{2,1,0:T(8,128)S(1)}, ...), condition=%wide.region_11.12_spmd.clone, body=%wide.region_8.11_spmd.clone.sunk | while | flops 827148288 | bytes 48833448 | solution.py:62
  199.0 3.7 %fusion.147 = (f32[16,192]{1,0:T(8,128)S(1)}, f32[512,16,192]{0,2,1:T(8,128)}) fusion(pred[192,512]{1,0:T(8,128)(4,1)S(1)} %compare_and_fusion.9, bf16[1,16,192,128]{3,2,1,0:T(8,128)(2,1)S(1)} %get-tuple-element.880, bf16[6,512,128]{2,1,0:T(8,128)(2,1)S(1)} %get-tuple-element.879, s32[]{:T(128)} %get-tuple-element.860), kind=kOutput, calls=%fused_computation.32.clone.1 | convolution fusion | flops 407368704 | bytes 7319556 | tf_op jit(solution)/shard_map/while/body/eval_jaxpr/hgrd,khd->hgrk/dot_general | solution.py:30
  202.8 5.4 %bitcast_add_fusion.15 = f32[1,16,192,128]{3,2,1,0:T(8,128)} fusion(f32[1,16,192,128]{3,2,1,0:T(8,128)} %get-tuple-element.863, f32[512,16,192]{0,2,1:T(8,128)} %get-tuple-element.818, f32[16,192]{1,0:T(8,128)S(1)} %bitcast.296, pred[192,512]{1,0:T(8,128)(4,1)S(1)} %compare_and_fusion.9, f32[16,192]{1,0:T(8,128)S(1)} %get-tuple-element.819, ...), kind=kOutput, calls=%fused_computation.37.clone.1 | convolution fusion | flops 411697152 | bytes 9691649 | tf_op jit(solution)/shard_map/while/body/eval_jaxpr/hgrk,khd->hgrd/dot_general | solution.py:39
  208.2 2.1 fusion.149
  210.5 3.7 %fusion.147 = (f32[16,192]{1,0:T(8,128)S(1)}, f32[512,16,192]{0,2,1:T(8,128)}) fusion(pred[192,512]{1,0:T(8,128)(4,1)S(1)} %compare_and_fusion.9, bf16[1,16,192,128]{3,2,1,0:T(8,128)(2,1)S(1)} %get-tuple-element.880, bf16[6,512,128]{2,1,0:T(8,128)(2,1)S(1)} %get-tuple-element.879, s32[]{:T(128)} %get-tuple-element.860), kind=kOutput, calls=%fused_computation.32.clone.1 | convolution fusion | flops 407368704 | bytes 7319556 | tf_op jit(solution)/shard_map/while/body/eval_jaxpr/hgrd,khd->hgrk/dot_general | solution.py:30
  214.2 5.6 %bitcast_add_fusion.15 = f32[1,16,192,128]{3,2,1,0:T(8,128)} fusion(f32[1,16,192,128]{3,2,1,0:T(8,128)} %get-tuple-element.863, f32[512,16,192]{0,2,1:T(8,128)} %get-tuple-element.818, f32[16,192]{1,0:T(8,128)S(1)} %bitcast.296, pred[192,512]{1,0:T(8,128)(4,1)S(1)} %compare_and_fusion.9, f32[16,192]{1,0:T(8,128)S(1)} %get-tuple-element.819, ...), kind=kOutput, calls=%fused_computation.37.clone.1 | convolution fusion | flops 411697152 | bytes 9691649 | tf_op jit(solution)/shard_map/while/body/eval_jaxpr/hgrk,khd->hgrd/dot_general | solution.py:39
  219.9 2.1 fusion.149
  222.2 3.8 %fusion.147 = (f32[16,192]{1,0:T(8,128)S(1)}, f32[512,16,192]{0,2,1:T(8,128)}) fusion(pred[192,512]{1,0:T(8,128)(4,1)S(1)} %compare_and_fusion.9, bf16[1,16,192,128]{3,2,1,0:T(8,128)(2,1)S(1)} %get-tuple-element.880, bf16[6,512,128]{2,1,0:T(8,128)(2,1)S(1)} %get-tuple-element.879, s32[]{:T(128)} %get-tuple-element.860), kind=kOutput, calls=%fused_computation.32.clone.1 | convolution fusion | flops 407368704 | bytes 7319556 | tf_op jit(solution)/shard_map/while/body/eval_jaxpr/hgrd,khd->hgrk/dot_general | solution.py:30
  225.9 5.6 %bitcast_add_fusion.15 = f32[1,16,192,128]{3,2,1,0:T(8,128)} fusion(f32[1,16,192,128]{3,2,1,0:T(8,128)} %get-tuple-element.863, f32[512,16,192]{0,2,1:T(8,128)} %get-tuple-element.818, f32[16,192]{1,0:T(8,128)S(1)} %bitcast.296, pred[192,512]{1,0:T(8,128)(4,1)S(1)} %compare_and_fusion.9, f32[16,192]{1,0:T(8,128)S(1)} %get-tuple-element.819, ...), kind=kOutput, calls=%fused_computation.37.clone.1 | convolution fusion | flops 411697152 | bytes 9691649 | tf_op jit(solution)/shard_map/while/body/eval_jaxpr/hgrk,khd->hgrd/dot_general | solution.py:39
  231.6 2.1 fusion.149
  233.9 3.8 %fusion.147 = (f32[16,192]{1,0:T(8,128)S(1)}, f32[512,16,192]{0,2,1:T(8,128)}) fusion(pred[192,512]{1,0:T(8,128)(4,1)S(1)} %compare_and_fusion.9, bf16[1,16,192,128]{3,2,1,0:T(8,128)(2,1)S(1)} %get-tuple-element.880, bf16[6,512,128]{2,1,0:T(8,128)(2,1)S(1)} %get-tuple-element.879, s32[]{:T(128)} %get-tuple-element.860), kind=kOutput, calls=%fused_computation.32.clone.1 | convolution fusion | flops 407368704 | bytes 7319556 | tf_op jit(solution)/shard_map/while/body/eval_jaxpr/hgrd,khd->hgrk/dot_general | solution.py:30
  237.6 5.6 %bitcast_add_fusion.15 = f32[1,16,192,128]{3,2,1,0:T(8,128)} fusion(f32[1,16,192,128]{3,2,1,0:T(8,128)} %get-tuple-element.863, f32[512,16,192]{0,2,1:T(8,128)} %get-tuple-element.818, f32[16,192]{1,0:T(8,128)S(1)} %bitcast.296, pred[192,512]{1,0:T(8,128)(4,1)S(1)} %compare_and_fusion.9, f32[16,192]{1,0:T(8,128)S(1)} %get-tuple-element.819, ...), kind=kOutput, calls=%fused_computation.37.clone.1 | convolution fusion | flops 411697152 | bytes 9691649 | tf_op jit(solution)/shard_map/while/body/eval_jaxpr/hgrk,khd->hgrd/dot_general | solution.py:39
  243.2 2.1 fusion.149
  245.5 3.8 %fusion.147 = (f32[16,192]{1,0:T(8,128)S(1)}, f32[512,16,192]{0,2,1:T(8,128)}) fusion(pred[192,512]{1,0:T(8,128)(4,1)S(1)} %compare_and_fusion.9, bf16[1,16,192,128]{3,2,1,0:T(8,128)(2,1)S(1)} %get-tuple-element.880, bf16[6,512,128]{2,1,0:T(8,128)(2,1)S(1)} %get-tuple-element.879, s32[]{:T(128)} %get-tuple-element.860), kind=kOutput, calls=%fused_computation.32.clone.1 | convolution fusion | flops 407368704 | bytes 7319556 | tf_op jit(solution)/shard_map/while/body/eval_jaxpr/hgrd,khd->hgrk/dot_general | solution.py:30
  249.3 5.6 %bitcast_add_fusion.15 = f32[1,16,192,128]{3,2,1,0:T(8,128)} fusion(f32[1,16,192,128]{3,2,1,0:T(8,128)} %get-tuple-element.863, f32[512,16,192]{0,2,1:T(8,128)} %get-tuple-element.818, f32[16,192]{1,0:T(8,128)S(1)} %bitcast.296, pred[192,512]{1,0:T(8,128)(4,1)S(1)} %compare_and_fusion.9, f32[16,192]{1,0:T(8,128)S(1)} %get-tuple-element.819, ...), kind=kOutput, calls=%fused_computation.37.clone.1 | convolution fusion | flops 411697152 | bytes 9691649 | tf_op jit(solution)/shard_map/while/body/eval_jaxpr/hgrk,khd->hgrd/dot_general | solution.py:39
  254.9 2.1 fusion.149
  257.2 3.8 %fusion.147 = (f32[16,192]{1,0:T(8,128)S(1)}, f32[512,16,192]{0,2,1:T(8,128)}) fusion(pred[192,512]{1,0:T(8,128)(4,1)S(1)} %compare_and_fusion.9, bf16[1,16,192,128]{3,2,1,0:T(8,128)(2,1)S(1)} %get-tuple-element.880, bf16[6,512,128]{2,1,0:T(8,128)(2,1)S(1)} %get-tuple-element.879, s32[]{:T(128)} %get-tuple-element.860), kind=kOutput, calls=%fused_computation.32.clone.1 | convolution fusion | flops 407368704 | bytes 7319556 | tf_op jit(solution)/shard_map/while/body/eval_jaxpr/hgrd,khd->hgrk/dot_general | solution.py:30
  261.0 5.6 %bitcast_add_fusion.15 = f32[1,16,192,128]{3,2,1,0:T(8,128)} fusion(f32[1,16,192,128]{3,2,1,0:T(8,128)} %get-tuple-element.863, f32[512,16,192]{0,2,1:T(8,128)} %get-tuple-element.818, f32[16,192]{1,0:T(8,128)S(1)} %bitcast.296, pred[192,512]{1,0:T(8,128)(4,1)S(1)} %compare_and_fusion.9, f32[16,192]{1,0:T(8,128)S(1)} %get-tuple-element.819, ...), kind=kOutput, calls=%fused_computation.37.clone.1 | convolution fusion | flops 411697152 | bytes 9691649 | tf_op jit(solution)/shard_map/while/body/eval_jaxpr/hgrk,khd->hgrd/dot_general | solution.py:39
  266.6 2.1 fusion.149
  268.7 1.9 divide_bitcast_fusion.1
  271.5 1.9 divide_bitcast_fusion
  274.7 1.3 pad_maximum_fusion
  275.9 2.5 fusion.114
  278.5 2.8 fusion.113
  281.3 21.7 %while.63 = (s32[]{:T(128)}, f32[1,16,32]{2,1,0:T(8,128)S(1)}, f32[1,16,32]{2,1,0:T(8,128)S(1)}, f32[1,16,32,128]{3,2,1,0:T(8,128)S(1)}, s32[7,512]{1,0:T(8,128)...) while((s32[]{:T(128)}, f32[1,16,32]{2,1,0:T(8,128)S(1)}, ...), condition=%wide.region_21.22_spmd.clone, body=%wide.region_18.21_spmd.clone.sunk | while | flops 136809504 | bytes 4170637 | solution.py:62
  281.4 1.3 fusion.158
  284.5 1.3 fusion.158
  287.6 1.3 fusion.158
  290.7 1.3 fusion.158
  293.8 1.3 fusion.158
  296.9 1.3 fusion.158
  300.0 1.3 fusion.158
  303.2 15.4 %while.62 = (s32[]{:T(128)}, f32[1,16,32]{2,1,0:T(8,128)S(1)}, f32[1,16,32]{2,1,0:T(8,128)S(1)}, f32[1,16,32,128]{3,2,1,0:T(8,128)S(1)}, s32[7,512]{1,0:T(8,128)...) while((s32[]{:T(128)}, f32[1,16,32]{2,1,0:T(8,128)S(1)}, ...), condition=%wide.region_16.17_spmd.clone, body=%wide.region_13.16_spmd.clone.sunk | while | flops 136809504 | bytes 4170129 | solution.py:62
  308.2 1.3 fusion.155
  (295 shorter events, 38.2 us)
Async XLA Ops:
  7.2 59.7 %all-gather.5.cloned.1.call-start = ((), (), s32[]{:S(2)}) async-start(), calls=%async_computation | async-start | bytes 1671168 | tf_op jit(solution)/shard_map/all_gather | solution.py:107
  7.9 112.4 %all-gather.7.cloned.1.call-start = ((), (), s32[]{:S(2)}) async-start(), calls=%async_computation.1 | async-start | bytes 1671168 | tf_op jit(solution)/shard_map/all_gather | solution.py:108
  8.6 267.3 %all-gather.9.cloned.1.call-start = ((), (), s32[]{:S(2)}) async-start(), calls=%async_computation.2 | async-start | bytes 1949696 | tf_op jit(solution)/shard_map/all_gather | solution.py:129
  10.3 268.2 %all-gather.11.cloned.1.call-start = ((), (), s32[]{:S(2)}) async-start(), calls=%async_computation.3 | async-start | bytes 1949696 | tf_op jit(solution)/shard_map/all_gather | solution.py:130
  16.9 1.7 copy-start.2
  127.9 5.5 %copy-start = (f32[512,16,192]{0,2,1:T(8,128)S(1)}, f32[512,16,192]{0,2,1:T(8,128)}, u32[]{:S(2)}) copy-start(f32[512,16,192]{0,2,1:T(8,128)} %get-tuple-element.804) | copy-start | bytes 18874372 | tf_op jit(solution)/shard_map/while
  140.3 5.7 %copy-start = (f32[512,16,192]{0,2,1:T(8,128)S(1)}, f32[512,16,192]{0,2,1:T(8,128)}, u32[]{:S(2)}) copy-start(f32[512,16,192]{0,2,1:T(8,128)} %get-tuple-element.804) | copy-start | bytes 18874372 | tf_op jit(solution)/shard_map/while
  153.0 5.7 %copy-start = (f32[512,16,192]{0,2,1:T(8,128)S(1)}, f32[512,16,192]{0,2,1:T(8,128)}, u32[]{:S(2)}) copy-start(f32[512,16,192]{0,2,1:T(8,128)} %get-tuple-element.804) | copy-start | bytes 18874372 | tf_op jit(solution)/shard_map/while
  165.6 5.7 %copy-start = (f32[512,16,192]{0,2,1:T(8,128)S(1)}, f32[512,16,192]{0,2,1:T(8,128)}, u32[]{:S(2)}) copy-start(f32[512,16,192]{0,2,1:T(8,128)} %get-tuple-element.804) | copy-start | bytes 18874372 | tf_op jit(solution)/shard_map/while
  178.3 5.7 %copy-start = (f32[512,16,192]{0,2,1:T(8,128)S(1)}, f32[512,16,192]{0,2,1:T(8,128)}, u32[]{:S(2)}) copy-start(f32[512,16,192]{0,2,1:T(8,128)} %get-tuple-element.804) | copy-start | bytes 18874372 | tf_op jit(solution)/shard_map/while
  191.0 5.7 %copy-start = (f32[512,16,192]{0,2,1:T(8,128)S(1)}, f32[512,16,192]{0,2,1:T(8,128)}, u32[]{:S(2)}) copy-start(f32[512,16,192]{0,2,1:T(8,128)} %get-tuple-element.804) | copy-start | bytes 18874372 | tf_op jit(solution)/shard_map/while
  202.7 5.4 %copy-start.1 = (f32[512,16,192]{0,2,1:T(8,128)S(1)}, f32[512,16,192]{0,2,1:T(8,128)}, u32[]{:S(2)}) copy-start(f32[512,16,192]{0,2,1:T(8,128)} %get-tuple-element.818) | copy-start | bytes 18874372 | tf_op jit(solution)/shard_map/while
  214.2 5.6 %copy-start.1 = (f32[512,16,192]{0,2,1:T(8,128)S(1)}, f32[512,16,192]{0,2,1:T(8,128)}, u32[]{:S(2)}) copy-start(f32[512,16,192]{0,2,1:T(8,128)} %get-tuple-element.818) | copy-start | bytes 18874372 | tf_op jit(solution)/shard_map/while
  225.9 5.6 %copy-start.1 = (f32[512,16,192]{0,2,1:T(8,128)S(1)}, f32[512,16,192]{0,2,1:T(8,128)}, u32[]{:S(2)}) copy-start(f32[512,16,192]{0,2,1:T(8,128)} %get-tuple-element.818) | copy-start | bytes 18874372 | tf_op jit(solution)/shard_map/while
  237.6 5.6 %copy-start.1 = (f32[512,16,192]{0,2,1:T(8,128)S(1)}, f32[512,16,192]{0,2,1:T(8,128)}, u32[]{:S(2)}) copy-start(f32[512,16,192]{0,2,1:T(8,128)} %get-tuple-element.818) | copy-start | bytes 18874372 | tf_op jit(solution)/shard_map/while
  249.3 5.6 %copy-start.1 = (f32[512,16,192]{0,2,1:T(8,128)S(1)}, f32[512,16,192]{0,2,1:T(8,128)}, u32[]{:S(2)}) copy-start(f32[512,16,192]{0,2,1:T(8,128)} %get-tuple-element.818) | copy-start | bytes 18874372 | tf_op jit(solution)/shard_map/while
  261.0 5.6 %copy-start.1 = (f32[512,16,192]{0,2,1:T(8,128)S(1)}, f32[512,16,192]{0,2,1:T(8,128)}, u32[]{:S(2)}) copy-start(f32[512,16,192]{0,2,1:T(8,128)} %get-tuple-element.818) | copy-start | bytes 18874372 | tf_op jit(solution)/shard_map/while
Sparse Core Ops, SparseCore 0:
  10.8 56.0 all-gather.4
  69.6 50.6 all-gather.6
  123.7 51.4 all-gather.8
  177.8 51.6 all-gather.10
where the time goes:
time: 327 us; the launch traced here: 326 us
  matrix products  147 us (45%)
  waiting for transfers between devices  95.4 us (29%)
  other arithmetic  49.8 us (15%)
  local copies, waits for them, and re-layouts  18 us (6%)
  between operations  14.2 us (4%)
    dot_general x26, matrix products, absorb(): jnp.einsum('hgrk,khd->hgrd', weights.astype(jnp.bfloat16), values3, prefe...  85.1 us
    dot_general x26, matrix products, absorb(): jnp.einsum('hgrd,khd->hgrk', query4, keys3, preferred_element_type=jnp.fl...  62.1 us
    all_gather x1, waiting for transfers between devices, on_device(): value_rows = lax.all_gather(v_prompt, 'ctx', axis=1, tiled=True)  51.1 us
    all_gather x1, waiting for transfers between devices, on_device(): key_rows = lax.all_gather(k_prompt, 'ctx', axis=1, tiled=True)  42.8 us
    reduce_sum x26, other arithmetic, absorb(): weight_sum = weight_sum * factor + jnp.sum(weights, axis=-1)  29.4 us
  transfers between devices with their start and end apart: 4, of which 2 were waited for; matrix products, arithmetic and copies ran while one was open for 53% of the time, Pallas kernels for 0%

commit v1 on v0

v1 whole, which is shorter than its diff:
```python
import functools
import math

import jax
import jax.numpy as jnp
from jax import lax
from jax.experimental import pallas as pl
from jax.experimental.pallas import tpu as pltpu
from jax.sharding import PartitionSpec as P

HEAD_DIM = 128
CONV = 2
HALF = 96
FOLLOW = 32
CHUNK = 2 * HALF + FOLLOW
GROUP = 16
CTX = 16
PROMPT_TILE = 384
PROMPT_HEADS = PROMPT_TILE // HALF
FOLLOW_TILE = 256
FOLLOW_HEADS = FOLLOW_TILE // FOLLOW
TILE_UNITS = 4
TILES = 5
HIDE = -1e30
FLOOR = -1e20
SCALE = math.log2(math.e) / math.sqrt(HEAD_DIM)
MESH = pl.DeviceIdType.MESH

SLOTS = (
    (0, 0, 0), (0, 0, 1), (3, 0, 0), (3, 0, 1), (1, 0, 0), (1, 0, 1), (0, 1, 0), (0, 1, 1),
    (3, 1, 0), (3, 1, 1), (1, 1, 0), (1, 1, 1), (2, 0, 0), (2, 0, 1), (2, 1, 0), (2, 1, 1),
)
SLOT_OF = {place: s for s, place in enumerate(SLOTS)}

OWN_SENDS = (
    ((0, 0, 0), 0, 2, (0, 1, 0), (0, 1, 0)),
    ((0, 0, 0), 0, 2, (1, 0, 0), (3, 0, 0)),
    ((0, 0, 0), 0, 2, (3, 0, 0), (1, 0, 0)),
    ((0, 0, 0), 0, 2, (0, 0, 1), (0, 0, 1)),
)
FORWARDS = {
    (0, 1, 0): (
        ((0, 1, 0), 0, 2, (1, 0, 0), (3, 1, 0)),
        ((0, 1, 0), 0, 2, (3, 0, 0), (1, 1, 0)),
        ((0, 1, 0), 0, 2, (0, 0, 1), (0, 1, 1)),
    ),
    (3, 0, 0): (
        ((3, 0, 0), 0, 1, (1, 0, 0), (2, 0, 0)),
        ((3, 0, 0), 0, 2, (0, 0, 1), (3, 0, 1)),
    ),
    (1, 0, 0): (
        ((1, 0, 0), 1, 1, (3, 0, 0), (2, 0, 0)),
        ((1, 0, 0), 0, 2, (0, 0, 1), (1, 0, 1)),
    ),
    (3, 1, 0): (
        ((3, 1, 0), 0, 1, (1, 0, 0), (2, 1, 0)),
        ((3, 1, 0), 0, 2, (0, 0, 1), (3, 1, 1)),
    ),
    (1, 1, 0): (
        ((1, 1, 0), 1, 1, (3, 0, 0), (2, 1, 0)),
        ((1, 1, 0), 0, 2, (0, 0, 1), (1, 1, 1)),
    ),
    (2, 0, 0): (((2, 0, 0), 0, 2, (0, 0, 1), (2, 0, 1)),),
    (2, 1, 0): (((2, 1, 0), 0, 2, (0, 0, 1), (2, 1, 1)),),
}
ALL_SENDS = OWN_SENDS + tuple(send for sends in FORWARDS.values() for send in sends)
SEND_INDEX = {send: n for n, send in enumerate(ALL_SENDS)}


def scores_of(query, keys):
    return lax.dot_general(
        query, keys, (((1,), (1,)), ((), ())), preferred_element_type=jnp.float32
    )


def absorb(query, keys, values, highest, total):
    scores = scores_of(query, keys)
    width = scores.shape[1]
    top = jnp.maximum(jnp.max(scores, axis=1, keepdims=True), FLOOR)
    if highest is None:
        top = jnp.broadcast_to(top, (scores.shape[0], 128))
    else:
        top = jnp.maximum(highest, top)
    weights = jnp.exp2((scores - jnp.tile(top, (1, width // 128))) * SCALE).astype(jnp.bfloat16)
    beside = jnp.concatenate([values, jnp.ones_like(values)], axis=1)
    added = jnp.dot(weights, beside, preferred_element_type=jnp.float32)
    if highest is not None:
        factor = jnp.exp2((highest - top) * SCALE)
        added = added + total * jnp.tile(factor, (1, 2))
    return top, added


def kernel(
    lengths, order, q_hbm, k_hbm, v_hbm, qf_hbm, kf_hbm, vf_hbm,
    out_hbm, outf_hbm,
    q_ref, k_ref, v_ref, qf_ref, kf_ref, vf_ref, out_ref, outf_ref,
    held0, held1, f_mask, unit_mask, p_query_mask, f_query_mask,
    high_top, high_total, step_top, step_total, f_top, f_total,
    in_sem, out_sem, send_sem, recv_sem,
):
    held = (held0, held1)
    me = lax.axis_index("ctx")
    my_x, my_y, my_k = me // 4, (me // 2) % 2, me % 2

    def device_at(offset):
        dx, dy, dk = offset
        return (((my_x + dx) % 4) * 2 + (my_y + dy) % 2) * 2 + (my_k + dk) % 2

    loads = []
    for c in range(CONV):
        for n, (src, dst) in enumerate(
            ((k_hbm, k_ref), (v_hbm, v_ref), (kf_hbm, kf_ref), (vf_hbm, vf_ref))
        ):
            loads.append(pltpu.make_async_copy(src.at[c], dst.at[c], in_sem.at[4 * c + n]))
    load_q = [
        pltpu.make_async_copy(q_hbm.at[c], q_ref.at[c], in_sem.at[8 + c]) for c in range(CONV)
    ]
    load_qf = pltpu.make_async_copy(qf_hbm, qf_ref, in_sem.at[10])
    for load in loads:
        load.start()
    load_qf.start()
    for load in load_q:
        load.start()

    barrier = pltpu.get_barrier_semaphore()
    for send in OWN_SENDS:
        pl.semaphore_signal(barrier, inc=1, device_id={"ctx": device_at(send[3])}, device_id_type=MESH)
    pl.semaphore_wait(barrier, len(OWN_SENDS))

    def copy_of(c, send):
        source, part, parts, target, landing = send
        where = pl.ds(part, parts)
        return pltpu.make_async_remote_copy(
            src_ref=held[c].at[SLOT_OF[source], where],
            dst_ref=held[c].at[SLOT_OF[landing], where],
            send_sem=send_sem.at[c, SEND_INDEX[send]],
            recv_sem=recv_sem.at[c, SEND_INDEX[send]],
            device_id={"ctx": device_at(target)},
            device_id_type=MESH,
        )

    block = [[order[c, 2 * me + half] for half in range(2)] for c in range(CONV)]
    low_half = [jnp.where(block[c][0] < block[c][1], 0, 1) for c in range(CONV)]
    low_block = [jnp.minimum(block[c][0], block[c][1]) for c in range(CONV)]
    for c in range(CONV):
        for load in loads[4 * c : 4 * c + 4]:
            load.wait()
        for part, (rows, later) in enumerate(((k_ref, kf_ref), (v_ref, vf_ref))):
            first, second = rows[c, 0], rows[c, 1]
            held[c][0, part, 0:HALF, :] = jnp.where(low_half[c] == 0, first, second)
            held[c][0, part, HALF : 2 * HALF, :] = jnp.where(low_half[c] == 0, second, first)
            held[c][0, part, 2 * HALF : CHUNK, :] = later[c]
        for send in OWN_SENDS:
            copy_of(c, send).start()

    def arrive(c, slot):
        for send in ALL_SENDS:
            if send[4] == slot:
                copy_of(c, send).wait_recv()
        for send in FORWARDS.get(slot, ()):
            copy_of(c, send).start()

    def iotas(rows):
        return (
            lax.broadcasted_iota(jnp.int32, (rows, 128), 0),
            lax.broadcasted_iota(jnp.int32, (rows, 128), 1),
        )

    row, lane = iotas(HALF)
    unit_mask[0] = jnp.zeros((HALF, 128), jnp.bfloat16)
    unit_mask[1] = jnp.where(lane == row, 1.0, 0.0).astype(jnp.bfloat16)
    unit_mask[2] = jnp.where(lane == HALF, 1.0, 0.0).astype(jnp.bfloat16)
    hidden = jnp.where(((lane > row) & (lane < HALF)) | (lane == HALF), HIDE, 0.0).astype(jnp.bfloat16)
    for h in range(PROMPT_HEADS):
        p_query_mask[h * HALF : (h + 1) * HALF, :] = hidden
    row, lane = iotas(FOLLOW)
    hidden = jnp.where(((lane > row) & (lane < FOLLOW)) | (lane == FOLLOW), HIDE, 0.0).astype(jnp.bfloat16)
    for h in range(FOLLOW_HEADS):
        f_query_mask[h * FOLLOW : (h + 1) * FOLLOW, :] = hidden
    for c in range(CONV):
        for slot, offset in enumerate(SLOTS):
            owner = device_at(offset)
            lower = jnp.minimum(order[c, 2 * owner], order[c, 2 * owner + 1])
            row, lane = iotas(HALF)
            for half, number in enumerate((lower, 31 - lower)):
                dead = (row + number * HALF >= lengths[c, 0]) & (lane == FOLLOW)
                f_mask[c, slot, half * HALF : (half + 1) * HALF, :] = jnp.where(dead, 1.0, 0.0).astype(
                    jnp.bfloat16
                )
            row, lane = iotas(FOLLOW)
            position = row + owner * FOLLOW
            if slot == 0:
                seen = (lane == row) | ((position >= lengths[c, 1]) & (lane == FOLLOW))
            else:
                last = jnp.minimum(lengths[c, 1], me * FOLLOW)
                seen = (position >= last) & (lane == FOLLOW)
            f_mask[c, slot, 2 * HALF : CHUNK, :] = jnp.where(seen, 1.0, 0.0).astype(jnp.bfloat16)

    def place(c, number):
        found = jnp.int32(0)
        for slot, offset in enumerate(SLOTS):
            owner = device_at(offset)
            lower = jnp.minimum(order[c, 2 * owner], order[c, 2 * owner + 1])
            found = jnp.where(lower == number, slot, found)
        return found

    def prompt_query(c, half, tile):
        start = tile * (PROMPT_HEADS * HEAD_DIM)
        return jnp.concatenate(
            [
                q_ref[c, half, :, pl.ds(pl.multiple_of(start + h * HEAD_DIM, HEAD_DIM), HEAD_DIM)]
                for h in range(PROMPT_HEADS)
            ],
            axis=0,
        )

    def high_on_low(c, slots, first):
        keys = [held[c][s, 0, 0:HALF, :] for s in slots]
        values = [held[c][s, 1, 0:HALF, :] for s in slots]

        def step(tile, carry):
            rows = pl.ds(pl.multiple_of(tile * PROMPT_TILE, PROMPT_TILE), PROMPT_TILE)
            query = prompt_query(c, 1 - low_half[c], tile)
            top, total = absorb(
                query,
                jnp.concatenate([held[c][s, 0, 0:HALF, :] for s in slots], axis=0),
                jnp.concatenate([held[c][s, 1, 0:HALF, :] for s in slots], axis=0),
                None if first else high_top[rows, :],
                None if first else high_total[rows, :],
            )
            high_top[rows, :] = top
            high_total[rows, :] = total
            return carry

        lax.fori_loop(0, GROUP // PROMPT_HEADS, step, 0)

    def follow(c, slots, first):
        def step(tile, carry):
            rows = pl.ds(pl.multiple_of(tile * FOLLOW_TILE, FOLLOW_TILE), FOLLOW_TILE)
            start = tile * (FOLLOW_HEADS * HEAD_DIM)
            query = jnp.concatenate(
                [
                    qf_ref[c, :, pl.ds(pl.multiple_of(start + h * HEAD_DIM, HEAD_DIM), HEAD_DIM)]
                    for h in range(FOLLOW_HEADS)
                ],
                axis=0,
            )
            query = jnp.concatenate([query, f_query_mask[...]], axis=1)
            keys = jnp.concatenate(
                [jnp.concatenate([held[c][s, 0], f_mask[c, s]], axis=1) for s in slots], axis=0
            )
            top, total = absorb(
                query,
                keys,
                jnp.concatenate([held[c][s, 1] for s in slots], axis=0),
                None if first else f_top[rows, :],
                None if first else f_total[rows, :],
            )
            f_top[rows, :] = top
            f_total[rows, :] = total
            return carry

        lax.fori_loop(0, GROUP // FOLLOW_HEADS, step, 0)

    def finish_follow(c):
        live = lax.broadcasted_iota(jnp.int32, (FOLLOW, HEAD_DIM), 0) + me * FOLLOW < lengths[c, 1]
        for h in range(GROUP):
            rows = pl.ds(h * FOLLOW, FOLLOW)
            result = f_total[rows, 0:HEAD_DIM] / f_total[rows, HEAD_DIM:]
            outf_ref[c, :, h * HEAD_DIM : (h + 1) * HEAD_DIM] = jnp.where(live, result, 0.0).astype(
                jnp.bfloat16
            )

    def rest(c):
        mine = low_block[c]
        low_tiles = mine // TILE_UNITS + 1

        plan = []
        for t in range(TILES):
            is_high = jnp.where(low_tiles <= t, 1, 0)
            units = []
            for w in range(TILE_UNITS):
                ahead = jnp.where(
                    is_high == 1,
                    15 - (TILE_UNITS * (t - low_tiles) + w) - mine,
                    mine - (TILE_UNITS * t + w),
                )
                number = jnp.where(is_high == 1, mine + ahead, mine - ahead)
                number = jnp.minimum(jnp.maximum(number, 0), CTX - 1)
                kind = jnp.where(ahead > 0, 0, jnp.where(ahead == 0, 1, 2))
                units.append((place(c, number), kind))
            half = jnp.where(is_high == 1, 1 - low_half[c], low_half[c])
            before = 0 if t == 0 else jnp.where(low_tiles == t, 1, t + 1)
            plan.append((is_high, half, before, units))

        def step(tile, carry):
            rows = pl.ds(pl.multiple_of(tile * PROMPT_TILE, PROMPT_TILE), PROMPT_TILE)
            step_top[0] = jnp.full((PROMPT_TILE, 128), FLOOR, jnp.float32)
            step_total[0] = jnp.zeros((PROMPT_TILE, 2 * HEAD_DIM), jnp.float32)
            step_top[1] = high_top[rows, :]
            step_total[1] = high_total[rows, :]
            for t, (is_high, half, before, units) in enumerate(plan):
                keys, values = [], []
                for slot, kind in units:
                    rows_of = [
                        jnp.where(
                            is_high == 1,
                            held[c][slot, part, HALF : 2 * HALF, :],
                            held[c][slot, part, 0:HALF, :],
                        )
                        for part in range(2)
                    ]
                    keys.append(jnp.concatenate([rows_of[0], unit_mask[kind]], axis=1))
                    values.append(rows_of[1])
                query = jnp.concatenate([prompt_query(c, half, tile), p_query_mask[...]], axis=1)
                top, total = absorb(
                    query,
                    jnp.concatenate(keys, axis=0),
                    jnp.concatenate(values, axis=0),
                    step_top[before],
                    step_total[before],
                )
                step_top[t + 2] = top
                step_total[t + 2] = total
            for half in range(2):
                last = jnp.where(low_half[c] == half, low_tiles + 1, TILES + 1)
                position = (
                    lax.broadcasted_iota(jnp.int32, (HALF, HEAD_DIM), 0) + block[c][half] * HALF
                )
                live = position < lengths[c, 0]
                for h in range(PROMPT_HEADS):
                    some = pl.ds(h * HALF, HALF)
                    result = step_total[last, some, 0:HEAD_DIM] / step_total[last, some, HEAD_DIM:]
                    start = pl.multiple_of((tile * PROMPT_HEADS + h) * HEAD_DIM, HEAD_DIM)
                    out_ref[c, half, :, pl.ds(start, HEAD_DIM)] = jnp.where(
                        live, result, 0.0
                    ).astype(jnp.bfloat16)
            return carry

        lax.fori_loop(0, GROUP // PROMPT_HEADS, step, 0)

    stores = []

    def store(src, dst, n):
        copy = pltpu.make_async_copy(src, dst, out_sem.at[n])
        copy.start()
        stores.append(copy)

    schedule(arrive, high_on_low, follow, finish_follow, rest, store, load_q, load_qf,
             out_ref, out_hbm, outf_ref, outf_hbm)
    for c in range(CONV):
        for send in ALL_SENDS:
            copy_of(c, send).wait_send()
    for copy in stores:
        copy.wait()


def schedule(arrive, high_on_low, follow, finish_follow, rest, store, load_q, load_qf,
             out_ref, out_hbm, outf_ref, outf_hbm):
    load_qf.wait()
    for load in load_q:
        load.wait()
    for c in range(CONV):
        for slot in ((0, 0, 1), (3, 0, 0), (1, 0, 0), (0, 1, 0), (3, 0, 1), (1, 0, 1), (0, 1, 1)):
            arrive(c, slot)
        follow(c, (0, 1, 2, 3), True)
        follow(c, (4, 5, 6, 7), False)
        for slot in ((3, 1, 0), (1, 1, 0), (2, 0, 0)):
            arrive(c, slot)
        high_on_low(c, (0, 1, 2, 3, 4, 5, 6, 7), True)
        for slot in ((2, 1, 0), (3, 1, 1), (1, 1, 1), (2, 0, 1), (2, 1, 1)):
            arrive(c, slot)
        high_on_low(c, (8, 9, 10, 11, 12, 13, 14, 15), False)
        follow(c, (8, 9, 10, 11), False)
        follow(c, (12, 13, 14, 15), False)
        finish_follow(c)
        store(outf_ref.at[c], outf_hbm.at[c], 2 + c)
        rest(c)
        store(out_ref.at[c], out_hbm.at[c], c)


def on_device(q_prompt, k_prompt, v_prompt, q_follow, k_follow, v_follow, lengths, block_order):
    width = GROUP * HEAD_DIM
    any_space = pl.BlockSpec(memory_space=pl.ANY)
    smem = pl.BlockSpec(memory_space=pltpu.SMEM)
    bf16, f32 = jnp.bfloat16, jnp.float32
    halves = (CONV, 2, HALF)
    out, out_follow = pl.pallas_call(
        kernel,
        out_shape=(
            jax.ShapeDtypeStruct(halves + (width,), bf16),
            jax.ShapeDtypeStruct((CONV, FOLLOW, width), bf16),
        ),
        in_specs=[smem, smem] + [any_space] * 6,
        out_specs=(any_space, any_space),
        scratch_shapes=[
            pltpu.VMEM(halves + (width,), bf16),
            pltpu.VMEM(halves + (HEAD_DIM,), bf16),
            pltpu.VMEM(halves + (HEAD_DIM,), bf16),
            pltpu.VMEM((CONV, FOLLOW, width), bf16),
            pltpu.VMEM((CONV, FOLLOW, HEAD_DIM), bf16),
            pltpu.VMEM((CONV, FOLLOW, HEAD_DIM), bf16),
            pltpu.VMEM(halves + (width,), bf16),
            pltpu.VMEM((CONV, FOLLOW, width), bf16),
            pltpu.VMEM((CTX, 2, CHUNK, HEAD_DIM), bf16),
            pltpu.VMEM((CTX, 2, CHUNK, HEAD_DIM), bf16),
            pltpu.VMEM((CONV, CTX, CHUNK, HEAD_DIM), bf16),
            pltpu.VMEM((3, HALF, HEAD_DIM), bf16),
            pltpu.VMEM((PROMPT_TILE, HEAD_DIM), bf16),
            pltpu.VMEM((FOLLOW_TILE, HEAD_DIM), bf16),
            pltpu.VMEM((GROUP * HALF, HEAD_DIM), f32),
            pltpu.VMEM((GROUP * HALF, 2 * HEAD_DIM), f32),
            pltpu.VMEM((TILES + 2, PROMPT_TILE, HEAD_DIM), f32),
            pltpu.VMEM((TILES + 2, PROMPT_TILE, 2 * HEAD_DIM), f32),
            pltpu.VMEM((GROUP * FOLLOW, HEAD_DIM), f32),
            pltpu.VMEM((GROUP * FOLLOW, 2 * HEAD_DIM), f32),
            pltpu.SemaphoreType.DMA((11,)),
            pltpu.SemaphoreType.DMA((4,)),
            pltpu.SemaphoreType.DMA((CONV, len(ALL_SENDS))),
            pltpu.SemaphoreType.DMA((CONV, len(ALL_SENDS))),
        ],
        compiler_params=pltpu.CompilerParams(
            collective_id=0, has_side_effects=True, vmem_limit_bytes=48 << 20
        ),
        cost_estimate=pl.CostEstimate(
            flops=7_400_000_000, bytes_accessed=8_000_000, transcendentals=15_000_000
        ),
    )(
        lengths,
        block_order,
        q_prompt.reshape(halves + (width,)),
        k_prompt.reshape(halves + (HEAD_DIM,)),
        v_prompt.reshape(halves + (HEAD_DIM,)),
        q_follow,
        k_follow,
        v_follow,
    )
    return out.reshape(q_prompt.shape), out_follow


def solution(mesh):
    return jax.shard_map(
        on_device,
        mesh=mesh,
        in_specs=(P("dp", "ctx", "tp"),) * 6 + (P("dp", None), P("dp", None)),
        out_specs=(P("dp", "ctx", "tp"), P("dp", "ctx", "tp")),
        check_vma=False,
    )
```

time: 327 us -> 77.8 us (0.24)
  matrix products: 147 us -> 0 us
  waiting for transfers between devices: 95.4 us -> 0 us
  Pallas kernels: 0 us -> 68.1 us
  other arithmetic: 49.8 us -> 0 us
  between operations: 14.2 us -> 0.66 us
  local copies, waits for them, and re-layouts: 18 us -> 8.77 us
    dot_general x52 -> x0, matrix products: 147 us -> none  [the longest x26 85.1 us: absorb(): jnp.einsum('hgrk,khd->hgrd', weights.astype(jnp.bfloat16), values3, prefe...]
    all_gather x4 -> x0, waiting for transfers between devices: 94 us -> none  [the longest x1 51.1 us: on_device(): value_rows = lax.all_gather(v_prompt, 'ctx', axis=1, tiled=True)]
    pallas_call x0 -> x1, Pallas kernels: none -> 68.1 us  [on_device(): pl.pallas_call(kernel, out_shape=(jax.ShapeDtypeStruct(halves + (width,),...]
    reduce_sum x29 -> x0, other arithmetic: 29.8 us -> none  [the longest x26 29.4 us: absorb(): weight_sum = weight_sum * factor + jnp.sum(weights, axis=-1)]
    slice x5 -> x0, local copies, waits for them, and re-layouts: 11.9 us -> none  [the longest x1 2.8 us: on_device(): value_rows[follow_c]]
    unnamed x12 -> x18, local copies, waits for them, and re-layouts: 2.36 us -> 8.77 us
    transpose x4 -> x0, other arithmetic: 4.05 us -> none  [finish(): flat = normed.transpose(2, 0, 1, 3).reshape(row_count, -1)]
    lt x4 -> x0, other arithmetic: 3.92 us -> none  [the longest x2 1.35 us: on_device(): key_live = key_positions < lengths[prompt_c, 0]]
  transfers between devices with their start and end apart: 4 -> 0, of which waited for: 2 -> 0; matrix products, arithmetic and copies ran while one was open for 53% -> 0% of each run, Pallas kernels for 0% -> 0%
where the time goes in v1:
time: 77.8 us; the launch traced here: 77.5 us
  Pallas kernels  68.1 us (88%)
  local copies, waits for them, and re-layouts  8.77 us (11%)
    pallas_call x1, Pallas kernels, on_device(): pl.pallas_call(kernel, out_shape=(jax.ShapeDtypeStruct(halves + (width,),...  68.1 us
    unnamed x18, local copies, waits for them, and re-layouts  8.77 us

profile of v1, /device:TPU:1, one launch (start us, length us, event | category | flops | bytes accessed | tf_op | source)
XLA Modules:
  0.0 77.5 jit_solution(10476934278242879236)
XLA Ops:
  0.6 0.0 copy-start
  0.6 1.4 %copy-done = bf16[2,192,2048]{2,1,0:T(8,128)(2,1)S(1)} copy-done((bf16[2,192,2048]{2,1,0:T(8,128)(2,1)S(1)}, bf16[2,192,2048]{2,1,0:T(8,128)(2,1)}, u32[]{:S(2)}) %copy-start) | copy-done | bytes 1572888
  2.0 0.0 copy-start.1
  2.0 0.9 %copy-done.1 = bf16[2,32,2048]{2,1,0:T(8,128)(2,1)S(1)} copy-done((bf16[2,32,2048]{2,1,0:T(8,128)(2,1)S(1)}, bf16[2,32,2048]{2,1,0:T(8,128)(2,1)}, u32[]{:S(2)}) %copy-start.1) | copy-done | bytes 262168
  3.0 0.0 copy-start.2
  3.0 0.9 %copy-done.2 = bf16[2,192,128]{2,1,0:T(8,128)(2,1)S(1)} copy-done((bf16[2,192,128]{2,1,0:T(8,128)(2,1)S(1)}, bf16[2,192,128]{2,1,0:T(8,128)(2,1)}, u32[]{:S(2)}) %copy-start.2) | copy-done | bytes 98328
  3.9 0.0 copy-start.3
  3.9 0.9 %copy-done.3 = bf16[2,192,128]{2,1,0:T(8,128)(2,1)S(1)} copy-done((bf16[2,192,128]{2,1,0:T(8,128)(2,1)S(1)}, bf16[2,192,128]{2,1,0:T(8,128)(2,1)}, u32[]{:S(2)}) %copy-start.3) | copy-done | bytes 98328
  4.8 0.0 copy-start.4
  4.8 0.7 copy-done.4
  5.5 0.0 copy-start.5
  5.5 0.7 copy-done.5
  6.2 0.0 copy-start.6
  6.2 0.7 copy-done.6
  6.9 0.0 copy-start.7
  6.9 0.7 copy-done.7
  7.6 68.1 %shard_map.95 = (bf16[2,2,96,2048]{3,2,1,0:T(8,128)(2,1)S(1)}, bf16[2,32,2048]{2,1,0:T(8,128)(2,1)S(1)}) custom-call(s32[2,2]{1,0:T(2,128)S(1)} %copy-done.6, s32[2,32]{1,0:T(2,128)S(1)} %copy-done.7, bf16[2,2,96,2048]{3,2,1,0:T(8,128)(2,1)S(1)} %bitcast.5, bf16[2,2,96,128]{3,2,1,0:T(8,128)(2,1)S(1)} %bitcast.6, bf16[2,2,96,128]{3,2,1,0:T(8,128)(2,1)S(1)} %bitcast.7, ...), custom_call_target="tpu_custom_call" | custom-call | flops 7400000000 | bytes 8000000 | tf_op jit(solution)/shard_map/pallas_call | solution.py:388
  75.6 1.1 %copy.12 = bf16[2,192,2048]{2,1,0:T(8,128)(2,1)} copy(bf16[2,192,2048]{2,1,0:T(8,128)(2,1)S(1)} %bitcast.4) | data formatting | bytes 3145728
  76.8 0.7 copy.13
Async XLA Ops:
  0.6 1.4 %copy-start = (bf16[2,192,2048]{2,1,0:T(8,128)(2,1)S(1)}, bf16[2,192,2048]{2,1,0:T(8,128)(2,1)}, u32[]{:S(2)}) copy-start(bf16[2,192,2048]{2,1,0:T(8,128)(2,1)} %param.8) | copy-start | bytes 4718596
  2.0 0.9 %copy-start.1 = (bf16[2,32,2048]{2,1,0:T(8,128)(2,1)S(1)}, bf16[2,32,2048]{2,1,0:T(8,128)(2,1)}, u32[]{:S(2)}) copy-start(bf16[2,32,2048]{2,1,0:T(8,128)(2,1)} %qf_hbm.1) | copy-start | bytes 786436
  3.0 0.9 %copy-start.2 = (bf16[2,192,128]{2,1,0:T(8,128)(2,1)S(1)}, bf16[2,192,128]{2,1,0:T(8,128)(2,1)}, u32[]{:S(2)}) copy-start(bf16[2,192,128]{2,1,0:T(8,128)(2,1)} %param.9) | copy-start | bytes 294916
  3.9 0.9 %copy-start.3 = (bf16[2,192,128]{2,1,0:T(8,128)(2,1)S(1)}, bf16[2,192,128]{2,1,0:T(8,128)(2,1)}, u32[]{:S(2)}) copy-start(bf16[2,192,128]{2,1,0:T(8,128)(2,1)} %param.10) | copy-start | bytes 294916
  4.8 0.7 copy-start.4
  5.5 0.7 copy-start.5
  6.2 0.7 copy-start.6
  6.9 0.7 copy-start.7

commit v2 on v1

v2 whole, which is shorter than its diff:
```python
import functools
import math

import jax
import jax.numpy as jnp
from jax import lax
from jax.experimental import pallas as pl
from jax.experimental.pallas import tpu as pltpu
from jax.sharding import PartitionSpec as P

HEAD_DIM = 128
CONV = 2
HALF = 96
FOLLOW = 32
CHUNK = 2 * HALF + FOLLOW
GROUP = 16
CTX = 16
PROMPT_TILE = 384
PROMPT_HEADS = PROMPT_TILE // HALF
FOLLOW_TILE = 256
FOLLOW_HEADS = FOLLOW_TILE // FOLLOW
REST_TILES = (8, 8, 4)
HIDE = -1e30
FLOOR = -1e20
SCALE = math.log2(math.e) / math.sqrt(HEAD_DIM)
MESH = pl.DeviceIdType.MESH

SLOTS = (
    (0, 0, 0), (0, 0, 1), (3, 0, 0), (3, 0, 1), (1, 0, 0), (1, 0, 1), (0, 1, 0), (0, 1, 1),
    (3, 1, 0), (3, 1, 1), (1, 1, 0), (1, 1, 1), (2, 0, 0), (2, 0, 1), (2, 1, 0), (2, 1, 1),
)
SLOT_OF = {place: s for s, place in enumerate(SLOTS)}

OWN_SENDS = (
    ((0, 0, 0), 0, 2, (0, 1, 0), (0, 1, 0)),
    ((0, 0, 0), 0, 2, (1, 0, 0), (3, 0, 0)),
    ((0, 0, 0), 0, 2, (3, 0, 0), (1, 0, 0)),
    ((0, 0, 0), 0, 2, (0, 0, 1), (0, 0, 1)),
)
FORWARDS = {
    (0, 1, 0): (
        ((0, 1, 0), 0, 2, (1, 0, 0), (3, 1, 0)),
        ((0, 1, 0), 0, 2, (3, 0, 0), (1, 1, 0)),
        ((0, 1, 0), 0, 2, (0, 0, 1), (0, 1, 1)),
    ),
    (3, 0, 0): (
        ((3, 0, 0), 0, 1, (1, 0, 0), (2, 0, 0)),
        ((3, 0, 0), 0, 2, (0, 0, 1), (3, 0, 1)),
    ),
    (1, 0, 0): (
        ((1, 0, 0), 1, 1, (3, 0, 0), (2, 0, 0)),
        ((1, 0, 0), 0, 2, (0, 0, 1), (1, 0, 1)),
    ),
    (3, 1, 0): (
        ((3, 1, 0), 0, 1, (1, 0, 0), (2, 1, 0)),
        ((3, 1, 0), 0, 2, (0, 0, 1), (3, 1, 1)),
    ),
    (1, 1, 0): (
        ((1, 1, 0), 1, 1, (3, 0, 0), (2, 1, 0)),
        ((1, 1, 0), 0, 2, (0, 0, 1), (1, 1, 1)),
    ),
    (2, 0, 0): (((2, 0, 0), 0, 2, (0, 0, 1), (2, 0, 1)),),
    (2, 1, 0): (((2, 1, 0), 0, 2, (0, 0, 1), (2, 1, 1)),),
}
ALL_SENDS = OWN_SENDS + tuple(send for sends in FORWARDS.values() for send in sends)
SEND_INDEX = {send: n for n, send in enumerate(ALL_SENDS)}


def scores_of(query, keys):
    return lax.dot_general(
        query, keys, (((1,), (1,)), ((), ())), preferred_element_type=jnp.float32
    )


def weigh(scores, highest):
    top = jnp.maximum(jnp.max(scores, axis=1, keepdims=True), FLOOR)
    if highest is None:
        top = jnp.broadcast_to(top, (scores.shape[0], 128))
        factor = None
    else:
        top = jnp.maximum(highest, top)
        factor = jnp.exp2((highest - top) * SCALE)
    width = scores.shape[1]
    spread = jnp.tile(top, (1, -(-width // 128)))[:, :width]
    return top, jnp.exp2((scores - spread) * SCALE).astype(jnp.bfloat16), factor


def run(items):
    steps, calls = [], [[]]
    for item in items:
        if callable(item):
            calls[-1].append(item)
        else:
            steps.append(item)
            calls.append([])

    def begin(n):
        for call in calls[n]:
            call()
        return scores_of(steps[n][0](), steps[n][1]())

    ahead = begin(0)
    for n, (_, _, values, before, after) in enumerate(steps):
        scores = ahead
        if n + 1 < len(steps):
            ahead = begin(n + 1)
        highest, total = before()
        top, weights, factor = weigh(scores, highest)
        rows = values()
        added = jnp.dot(
            weights,
            jnp.concatenate([rows, jnp.ones_like(rows)], axis=1),
            preferred_element_type=jnp.float32,
        )
        if total is not None:
            added = added + total * jnp.tile(factor, (1, 2))
        after(top, added)
    for call in calls[-1]:
        call()


def kernel(
    lengths, order, q_hbm, k_hbm, v_hbm, qf_hbm, kf_hbm, vf_hbm,
    out_hbm, outf_hbm,
    q_ref, k_ref, v_ref, qf_ref, kf_ref, vf_ref, out_ref, outf_ref,
    held0, held1, f_mask, unit_mask, p_query_mask, f_query_mask,
    step_top, step_total, f_top, f_total,
    in_sem, out_sem, send_sem, recv_sem,
):
    held = (held0, held1)
    me = lax.axis_index("ctx")
    my_x, my_y, my_k = me // 4, lax.rem(me // 2, 2), lax.rem(me, 2)

    devices = {
        (dx, dy, dk): (lax.rem(my_x + dx, 4) * 2 + lax.rem(my_y + dy, 2)) * 2 + lax.rem(my_k + dk, 2)
        for dx, dy, dk in SLOTS
    }

    barrier = pltpu.get_barrier_semaphore()
    for send in OWN_SENDS:
        pl.semaphore_signal(barrier, inc=1, device_id={"ctx": devices[send[3]]}, device_id_type=MESH)

    loads = []
    for c in range(CONV):
        for n, (src, dst) in enumerate(
            ((k_hbm, k_ref), (v_hbm, v_ref), (kf_hbm, kf_ref), (vf_hbm, vf_ref))
        ):
            loads.append(pltpu.make_async_copy(src.at[c], dst.at[c], in_sem.at[4 * c + n]))
    load_q = [
        pltpu.make_async_copy(q_hbm.at[c], q_ref.at[c], in_sem.at[8 + c]) for c in range(CONV)
    ]
    load_qf = pltpu.make_async_copy(qf_hbm, qf_ref, in_sem.at[10])
    for load in loads:
        load.start()
    load_qf.start()
    for load in load_q:
        load.start()

    def copy_of(c, send):
        source, part, parts, target, landing = send
        where = pl.ds(part, parts)
        return pltpu.make_async_remote_copy(
            src_ref=held[c].at[SLOT_OF[source], where],
            dst_ref=held[c].at[SLOT_OF[landing], where],
            send_sem=send_sem.at[c, SEND_INDEX[send]],
            recv_sem=recv_sem.at[c, SEND_INDEX[send]],
            device_id={"ctx": devices[target]},
            device_id_type=MESH,
        )

    block = [[order[c, 2 * me + half] for half in range(2)] for c in range(CONV)]
    low_half = [jnp.where(block[c][0] < block[c][1], 0, 1) for c in range(CONV)]
    low_block = [jnp.minimum(block[c][0], block[c][1]) for c in range(CONV)]
    for c in range(CONV):
        for load in loads[4 * c : 4 * c + 4]:
            load.wait()
        for part, (rows, later) in enumerate(((k_ref, kf_ref), (v_ref, vf_ref))):
            first, second = rows[c, 0], rows[c, 1]
            held[c][0, part, 0:HALF, :] = jnp.where(low_half[c] == 0, first, second)
            held[c][0, part, HALF : 2 * HALF, :] = jnp.where(low_half[c] == 0, second, first)
            held[c][0, part, 2 * HALF : CHUNK, :] = later[c]

    def arrive(c, slot):
        for send in ALL_SENDS:
            if send[4] == slot:
                copy_of(c, send).wait_recv()
        for send in FORWARDS.get(slot, ()):
            copy_of(c, send).start()

    step_top[0] = jnp.full((GROUP * HALF, 128), FLOOR, jnp.float32)
    step_total[0] = jnp.zeros((GROUP * HALF, 2 * HEAD_DIM), jnp.float32)

    def iotas(rows):
        return (
            lax.broadcasted_iota(jnp.int32, (rows, 128), 0),
            lax.broadcasted_iota(jnp.int32, (rows, 128), 1),
        )

    row, lane = iotas(HALF)
    unit_mask[0] = jnp.zeros((HALF, 128), jnp.bfloat16)
    unit_mask[1] = jnp.where(lane == row, 1.0, 0.0).astype(jnp.bfloat16)
    unit_mask[2] = jnp.where(lane == HALF, 1.0, 0.0).astype(jnp.bfloat16)
    hidden = jnp.where(((lane > row) & (lane < HALF)) | (lane == HALF), HIDE, 0.0).astype(jnp.bfloat16)
    for h in range(PROMPT_HEADS):
        p_query_mask[h * HALF : (h + 1) * HALF, :] = hidden
    row, lane = iotas(FOLLOW)
    hidden = jnp.where(((lane > row) & (lane < FOLLOW)) | (lane == FOLLOW), HIDE, 0.0).astype(jnp.bfloat16)
    for h in range(FOLLOW_HEADS):
        f_query_mask[h * FOLLOW : (h + 1) * FOLLOW, :] = hidden
    for c in range(CONV):
        for slot, offset in enumerate(SLOTS):
            owner = devices[offset]
            lower = jnp.minimum(order[c, 2 * owner], order[c, 2 * owner + 1])
            row, lane = iotas(HALF)
            for half, number in enumerate((lower, 31 - lower)):
                dead = (row + number * HALF >= lengths[c, 0]) & (lane == FOLLOW)
                f_mask[c, slot, half * HALF : (half + 1) * HALF, :] = jnp.where(dead, 1.0, 0.0).astype(
                    jnp.bfloat16
                )
            row, lane = iotas(FOLLOW)
            position = row + owner * FOLLOW
            if slot == 0:
                seen = (lane == row) | ((position >= lengths[c, 1]) & (lane == FOLLOW))
            else:
                last = jnp.minimum(lengths[c, 1], me * FOLLOW)
                seen = (position >= last) & (lane == FOLLOW)
            f_mask[c, slot, 2 * HALF : CHUNK, :] = jnp.where(seen, 1.0, 0.0).astype(jnp.bfloat16)

    pl.semaphore_wait(barrier, len(OWN_SENDS))
    for c in range(CONV):
        for send in OWN_SENDS:
            copy_of(c, send).start()

    def place(c, number):
        found = jnp.int32(0)
        for slot, offset in enumerate(SLOTS):
            owner = devices[offset]
            lower = jnp.minimum(order[c, 2 * owner], order[c, 2 * owner + 1])
            found = jnp.where(lower == number, slot, found)
        return found

    def prompt_query(c, half, tile):
        start = tile * (PROMPT_HEADS * HEAD_DIM)
        return jnp.concatenate(
            [
                q_ref[c, half, :, start + h * HEAD_DIM : start + (h + 1) * HEAD_DIM]
                for h in range(PROMPT_HEADS)
            ],
            axis=0,
        )

    def state(tops, totals, rows, first):
        def before():
            return (None, None) if first else (tops[rows, :], totals[rows, :])

        def after(top, total):
            tops[rows, :] = top
            totals[rows, :] = total

        return before, after

    def high_on_low(c, slots, first):
        units = []
        for tile in range(GROUP // PROMPT_HEADS):
            rows = pl.ds(tile * PROMPT_TILE, PROMPT_TILE)
            units.append(
                (
                    functools.partial(prompt_query, c, 1 - low_half[c], tile),
                    lambda: jnp.concatenate([held[c][s, 0, 0:HALF, :] for s in slots], axis=0),
                    lambda: jnp.concatenate([held[c][s, 1, 0:HALF, :] for s in slots], axis=0),
                )
                + state(step_top.at[1 + c], step_total.at[1 + c], rows, first)
            )
        return units

    def follow(c, slots, first):
        units = []
        for tile in range(GROUP // FOLLOW_HEADS):
            rows = pl.ds(tile * FOLLOW_TILE, FOLLOW_TILE)

            def query(start=tile * FOLLOW_HEADS * HEAD_DIM):
                heads = [
                    qf_ref[c, :, start + h * HEAD_DIM : start + (h + 1) * HEAD_DIM]
                    for h in range(FOLLOW_HEADS)
                ]
                return jnp.concatenate([jnp.concatenate(heads, axis=0), f_query_mask[...]], axis=1)

            units.append(
                (
                    query,
                    lambda: jnp.concatenate(
                        [jnp.concatenate([held[c][s, 0], f_mask[c, s]], axis=1) for s in slots],
                        axis=0,
                    ),
                    lambda: jnp.concatenate([held[c][s, 1] for s in slots], axis=0),
                )
                + state(f_top.at[c], f_total.at[c], rows, first)
            )
        return units

    stores = []

    def store(src, dst):
        copy = pltpu.make_async_copy(src, dst, out_sem.at[len(stores)])
        copy.start()
        stores.append(copy)

    def finish_follow(c):
        live = lax.broadcasted_iota(jnp.int32, (FOLLOW, HEAD_DIM), 0) + me * FOLLOW < lengths[c, 1]
        for h in range(GROUP):
            rows = pl.ds(h * FOLLOW, FOLLOW)
            result = f_total[c, rows, 0:HEAD_DIM] / f_total[c, rows, HEAD_DIM:]
            outf_ref[c, :, h * HEAD_DIM : (h + 1) * HEAD_DIM] = jnp.where(live, result, 0.0).astype(
                jnp.bfloat16
            )
        store(outf_ref.at[c], outf_hbm.at[c])

    def rest(c):
        mine = low_block[c]
        case = mine // 4

        def pick(*by_case):
            return jnp.where(
                case == 0, by_case[0], jnp.where(case == 1, by_case[1], jnp.where(case == 2, by_case[2], by_case[3]))
            )

        is_high = (pick(1, 0, 0, 0), pick(1, 1, 1, 0), pick(0, 1, 0, 1))
        offset = (0, pick(8, 0, 0, 8), pick(0, 8, 8, 0))
        begun = 1 + c
        before_of = (pick(begun, 0, 0, 0), pick(3, begun, begun, 3), pick(0, 4, 3, begun))
        last_low, last_high = pick(5, 3, 5, 4), pick(4, 5, 4, 5)
        units = []
        for t, size in enumerate(REST_TILES):
            blocks = []
            for w in range(size):
                reach = jnp.where(is_high[t] == 1, 15 - mine, mine)
                ahead = reach - (offset[t] + w)
                number = jnp.where(is_high[t] == 1, mine + ahead, mine - ahead)
                number = jnp.minimum(jnp.maximum(number, 0), CTX - 1)
                kind = jnp.where(ahead > 0, 0, jnp.where(ahead == 0, 1, 2))
                blocks.append((place(c, number), kind))
            half = jnp.where(is_high[t] == 1, 1 - low_half[c], low_half[c])

            def rows_of(slot, part, high=is_high[t]):
                return jnp.where(
                    high == 1, held[c][slot, part, HALF : 2 * HALF, :], held[c][slot, part, 0:HALF, :]
                )

            def keys(blocks=blocks, rows_of=rows_of):
                return jnp.concatenate(
                    [
                        jnp.concatenate([rows_of(slot, 0), unit_mask[kind]], axis=1)
                        for slot, kind in blocks
                    ],
                    axis=0,
                )

            def values(blocks=blocks, rows_of=rows_of):
                return jnp.concatenate([rows_of(slot, 1) for slot, _ in blocks], axis=0)

            for tile in range(GROUP // PROMPT_HEADS):
                rows = pl.ds(tile * PROMPT_TILE, PROMPT_TILE)

                def query(half=half, tile=tile):
                    return jnp.concatenate([prompt_query(c, half, tile), p_query_mask[...]], axis=1)

                def before(t=t, rows=rows):
                    return step_top[before_of[t], rows, :], step_total[before_of[t], rows, :]

                def after(top, total, t=t, rows=rows):
                    step_top[t + 3, rows, :] = top
                    step_total[t + 3, rows, :] = total

                units.append((query, keys, values, before, after))

        def finish(tile):
            for half in range(2):
                last = jnp.where(low_half[c] == half, last_low, last_high)
                position = (
                    lax.broadcasted_iota(jnp.int32, (HALF, HEAD_DIM), 0) + block[c][half] * HALF
                )
                live = position < lengths[c, 0]
                for h in range(tile * PROMPT_HEADS, (tile + 1) * PROMPT_HEADS):
                    rows = pl.ds(h * HALF, HALF)
                    result = step_total[last, rows, 0:HEAD_DIM] / step_total[last, rows, HEAD_DIM:]
                    out_ref[c, half, :, h * HEAD_DIM : (h + 1) * HEAD_DIM] = jnp.where(
                        live, result, 0.0
                    ).astype(jnp.bfloat16)
            columns = pl.ds(tile * PROMPT_HEADS * HEAD_DIM, PROMPT_HEADS * HEAD_DIM)
            store(out_ref.at[c, :, :, columns], out_hbm.at[c, :, :, columns])

        finishes = [functools.partial(finish, tile) for tile in range(GROUP // PROMPT_HEADS)]
        return units, finishes

    schedule(arrive, high_on_low, follow, finish_follow, rest, load_q, load_qf)
    for c in range(CONV):
        for send in ALL_SENDS:
            copy_of(c, send).wait_send()
    for copy in stores:
        copy.wait()


def schedule(arrive, high_on_low, follow, finish_follow, rest, load_q, load_qf):
    near = (0, 1, 2, 3, 4, 5, 6, 7)
    middle = (8, 9, 10, 11, 12, 13)
    last = (14, 15)
    far = middle + last

    def wait_for(c, *slots):
        def call():
            for slot in slots:
                arrive(c, slot)

        return call

    first = ((3, 0, 0), (1, 0, 0), (0, 1, 0))
    first_shared = ((0, 0, 1), (3, 0, 1), (1, 0, 1), (0, 1, 1))
    second = ((3, 1, 0), (1, 1, 0))
    middle_shared = ((3, 1, 1), (1, 1, 1), (2, 0, 1))
    load_qf.wait()
    for load in load_q:
        load.wait()
    h, f = high_on_low(0, near, True), follow(0, near, True)
    items = [wait_for(0, *first), wait_for(0, *first_shared)]
    items += h[:2] + [wait_for(1, *first)] + h[2:] + f
    h, f = high_on_low(1, near, True), follow(1, near, True)
    items += [wait_for(1, *first_shared), wait_for(0, (2, 0, 0))]
    items += h[:3] + [wait_for(0, *second)] + h[3:] + [wait_for(1, (2, 0, 0))] + f
    h, f = high_on_low(0, middle, False), follow(0, middle, False)
    items += [wait_for(0, *middle_shared)]
    items += h[:2] + [wait_for(1, *second)] + h[2:] + f[:1] + [wait_for(0, (2, 1, 0))] + f[1:]
    h, f = high_on_low(0, last, False), follow(0, last, False)
    items += [wait_for(0, (2, 1, 1))] + h + f + [wait_for(1, (2, 1, 0))]
    units, finishes = rest(0)
    items += units[:4] + [functools.partial(finish_follow, 0)] + units[4:10] + finishes[:1]
    items += units[10:11] + finishes[1:2] + units[11:]
    h, f = high_on_low(1, far, False), follow(1, far, False)
    items += [wait_for(1, *middle_shared, (2, 1, 1))]
    items += f[:1] + finishes[2:3] + f[1:] + finishes[3:] + h
    units, finishes = rest(1)
    items += units[:4] + [functools.partial(finish_follow, 1)] + units[4:10] + finishes[:1]
    items += units[10:11] + finishes[1:2] + units[11:] + finishes[2:]
    run(items)


def on_device(q_prompt, k_prompt, v_prompt, q_follow, k_follow, v_follow, lengths, block_order):
    width = GROUP * HEAD_DIM
    any_space = pl.BlockSpec(memory_space=pl.ANY)
    smem = pl.BlockSpec(memory_space=pltpu.SMEM)
    bf16, f32 = jnp.bfloat16, jnp.float32
    halves = (CONV, 2, HALF)
    out, out_follow = pl.pallas_call(
        kernel,
        out_shape=(
            jax.ShapeDtypeStruct(halves + (width,), bf16),
            jax.ShapeDtypeStruct((CONV, FOLLOW, width), bf16),
        ),
        in_specs=[smem, smem] + [any_space] * 6,
        out_specs=(any_space, any_space),
        scratch_shapes=[
            pltpu.VMEM(halves + (width,), bf16),
            pltpu.VMEM(halves + (HEAD_DIM,), bf16),
            pltpu.VMEM(halves + (HEAD_DIM,), bf16),
            pltpu.VMEM((CONV, FOLLOW, width), bf16),
            pltpu.VMEM((CONV, FOLLOW, HEAD_DIM), bf16),
            pltpu.VMEM((CONV, FOLLOW, HEAD_DIM), bf16),
            pltpu.VMEM(halves + (width,), bf16),
            pltpu.VMEM((CONV, FOLLOW, width), bf16),
            pltpu.VMEM((CTX, 2, CHUNK, HEAD_DIM), bf16),
            pltpu.VMEM((CTX, 2, CHUNK, HEAD_DIM), bf16),
            pltpu.VMEM((CONV, CTX, CHUNK, HEAD_DIM), bf16),
            pltpu.VMEM((3, HALF, HEAD_DIM), bf16),
            pltpu.VMEM((PROMPT_TILE, HEAD_DIM), bf16),
            pltpu.VMEM((FOLLOW_TILE, HEAD_DIM), bf16),
            pltpu.VMEM((1 + CONV + len(REST_TILES), GROUP * HALF, HEAD_DIM), f32),
            pltpu.VMEM((1 + CONV + len(REST_TILES), GROUP * HALF, 2 * HEAD_DIM), f32),
            pltpu.VMEM((CONV, GROUP * FOLLOW, HEAD_DIM), f32),
            pltpu.VMEM((CONV, GROUP * FOLLOW, 2 * HEAD_DIM), f32),
            pltpu.SemaphoreType.DMA((11,)),
            pltpu.SemaphoreType.DMA((CONV + CONV * (GROUP // PROMPT_HEADS),)),
            pltpu.SemaphoreType.DMA((CONV, len(ALL_SENDS))),
            pltpu.SemaphoreType.DMA((CONV, len(ALL_SENDS))),
        ],
        compiler_params=pltpu.CompilerParams(
            collective_id=0, has_side_effects=True, vmem_limit_bytes=63 << 20
        ),
        cost_estimate=pl.CostEstimate(
            flops=7_400_000_000, bytes_accessed=8_000_000, transcendentals=15_000_000
        ),
    )(
        lengths,
        block_order,
        q_prompt.reshape(halves + (width,)),
        k_prompt.reshape(halves + (HEAD_DIM,)),
        v_prompt.reshape(halves + (HEAD_DIM,)),
        q_follow,
        k_follow,
        v_follow,
    )
    return out.reshape(q_prompt.shape), out_follow


def solution(mesh):
    return jax.shard_map(
        on_device,
        mesh=mesh,
        in_specs=(P("dp", "ctx", "tp"),) * 6 + (P("dp", None), P("dp", None)),
        out_specs=(P("dp", "ctx", "tp"), P("dp", "ctx", "tp")),
        check_vma=False,
    )
```

time: 77.8 us -> 46.6 us (0.60)
  Pallas kernels: 68.1 us -> 42.3 us
  local copies, waits for them, and re-layouts: 8.77 us -> 3.48 us
    pallas_call x1, Pallas kernels: 68.1 us -> 42.3 us  [on_device(): pl.pallas_call(kernel, out_shape=(jax.ShapeDtypeStruct(halves + (width,),...]
    unnamed x18 -> x4, local copies, waits for them, and re-layouts: 8.77 us -> 3.48 us
where the time goes in v2:
time: 46.6 us; the launch traced here: 46.4 us
  Pallas kernels  42.3 us (91%)
  local copies, waits for them, and re-layouts  3.48 us (7%)
  between operations  0.65 us (1%)
    pallas_call x1, Pallas kernels, on_device(): pl.pallas_call(kernel, out_shape=(jax.ShapeDtypeStruct(halves + (width,),...  42.3 us
    unnamed x4, local copies, waits for them, and re-layouts  3.48 us

profile of v2, /device:TPU:1, one launch (start us, length us, event | category | flops | bytes accessed | tf_op | source)
XLA Modules:
  0.0 46.4 jit_solution(7183159456517452280)
XLA Ops:
  0.6 42.3 %shard_map.95 = (bf16[2,2,96,2048]{3,2,1,0:T(8,128)(2,1)}, bf16[2,32,2048]{2,1,0:T(8,128)(2,1)}) custom-call(s32[2,2]{1,0:T(2,128)} %lengths.1, s32[2,32]{1,0:T(2,128)} %order.1, bf16[2,2,96,2048]{3,2,1,0:T(8,128)(2,1)} %bitcast.5, bf16[2,2,96,128]{3,2,1,0:T(8,128)(2,1)} %bitcast.6, bf16[2,2,96,128]{3,2,1,0:T(8,128)(2,1)} %bitcast.7, ...), custom_call_target="tpu_custom_call" | custom-call | flops 7400000000 | bytes 8000000 | tf_op jit(solution)/shard_map/pallas_call | solution.py:452
  42.9 0.0 copy-start
  42.9 2.8 %copy.12 = bf16[2,192,2048]{2,1,0:T(8,128)(2,1)} copy(bf16[2,192,2048]{2,1,0:T(8,128)(2,1)} %bitcast.4) | data formatting | bytes 3145728
  45.7 0.0 copy-done
  45.7 0.7 %copy.13 = bf16[2,32,2048]{2,1,0:T(8,128)(2,1)} copy(bf16[2,32,2048]{2,1,0:T(8,128)(2,1)S(1)} %copy-done) | data formatting | bytes 524288
Async XLA Ops:
  42.9 2.8 %copy-start = (bf16[2,32,2048]{2,1,0:T(8,128)(2,1)S(1)}, bf16[2,32,2048]{2,1,0:T(8,128)(2,1)}, u32[]{:S(2)}) copy-start(bf16[2,32,2048]{2,1,0:T(8,128)(2,1)} %get-tuple-element.9) | copy-start | bytes 786436

commit v3 on v2

--- a/solution.py
+++ b/solution.py
@@ -25,44 +25,33 @@
 SCALE = math.log2(math.e) / math.sqrt(HEAD_DIM)
 MESH = pl.DeviceIdType.MESH
 
-SLOTS = (
-    (0, 0, 0), (0, 0, 1), (3, 0, 0), (3, 0, 1), (1, 0, 0), (1, 0, 1), (0, 1, 0), (0, 1, 1),
-    (3, 1, 0), (3, 1, 1), (1, 1, 0), (1, 1, 1), (2, 0, 0), (2, 0, 1), (2, 1, 0), (2, 1, 1),
-)
-SLOT_OF = {place: s for s, place in enumerate(SLOTS)}
-
-OWN_SENDS = (
-    ((0, 0, 0), 0, 2, (0, 1, 0), (0, 1, 0)),
-    ((0, 0, 0), 0, 2, (1, 0, 0), (3, 0, 0)),
-    ((0, 0, 0), 0, 2, (3, 0, 0), (1, 0, 0)),
-    ((0, 0, 0), 0, 2, (0, 0, 1), (0, 0, 1)),
-)
-FORWARDS = {
-    (0, 1, 0): (
-        ((0, 1, 0), 0, 2, (1, 0, 0), (3, 1, 0)),
-        ((0, 1, 0), 0, 2, (3, 0, 0), (1, 1, 0)),
-        ((0, 1, 0), 0, 2, (0, 0, 1), (0, 1, 1)),
+CHIPS = ((0, 0), (3, 0), (1, 0), (0, 1), (3, 1), (1, 1), (2, 0), (2, 1))
+PLACES = tuple(chip + (dk,) for dk in range(2) for chip in CHIPS)
+SHARED = len(CHIPS)
+RIGHT, LEFT, ACROSS, BESIDE = (1, 0, 0), (3, 0, 0), (0, 1, 0), (0, 0, 1)
+
+SENDS = {
+    "own": (
+        (0, 1, 0, 2, RIGHT, 1),
+        (0, 1, 0, 2, LEFT, 2),
+        (0, 1, 0, 2, ACROSS, 3),
+        (0, 1, 0, 2, BESIDE, SHARED),
     ),
-    (3, 0, 0): (
-        ((3, 0, 0), 0, 1, (1, 0, 0), (2, 0, 0)),
-        ((3, 0, 0), 0, 2, (0, 0, 1), (3, 0, 1)),
+    "first": (
+        (3, 1, 0, 2, RIGHT, 4),
+        (3, 1, 0, 2, LEFT, 5),
+        (1, 1, 0, 1, RIGHT, 6),
+        (2, 1, 1, 1, LEFT, 6),
+        (1, 3, 0, 2, BESIDE, SHARED + 1),
     ),
-    (1, 0, 0): (
-        ((1, 0, 0), 1, 1, (3, 0, 0), (2, 0, 0)),
-        ((1, 0, 0), 0, 2, (0, 0, 1), (1, 0, 1)),
+    "second": (
+        (4, 1, 0, 1, RIGHT, 7),
+        (5, 1, 1, 1, LEFT, 7),
+        (4, 3, 0, 2, BESIDE, SHARED + 4),
     ),
-    (3, 1, 0): (
-        ((3, 1, 0), 0, 1, (1, 0, 0), (2, 1, 0)),
-        ((3, 1, 0), 0, 2, (0, 0, 1), (3, 1, 1)),
-    ),
-    (1, 1, 0): (
-        ((1, 1, 0), 1, 1, (3, 0, 0), (2, 1, 0)),
-        ((1, 1, 0), 0, 2, (0, 0, 1), (1, 1, 1)),
-    ),
-    (2, 0, 0): (((2, 0, 0), 0, 2, (0, 0, 1), (2, 0, 1)),),
-    (2, 1, 0): (((2, 1, 0), 0, 2, (0, 0, 1), (2, 1, 1)),),
+    "third": ((7, 1, 0, 2, BESIDE, SHARED + 7),),
 }
-ALL_SENDS = OWN_SENDS + tuple(send for sends in FORWARDS.values() for send in sends)
+ALL_SENDS = tuple(send for sends in SENDS.values() for send in sends)
 SEND_INDEX = {send: n for n, send in enumerate(ALL_SENDS)}
 
 
@@ -121,11 +110,11 @@
 
 def kernel(
     lengths, order, q_hbm, k_hbm, v_hbm, qf_hbm, kf_hbm, vf_hbm,
-    out_hbm, outf_hbm,
-    q_ref, k_ref, v_ref, qf_ref, kf_ref, vf_ref, out_ref, outf_ref,
+    out_ref, outf_ref,
+    q_ref, k_ref, v_ref, qf_ref, kf_ref, vf_ref,
     held0, held1, f_mask, unit_mask, p_query_mask, f_query_mask,
     step_top, step_total, f_top, f_total,
-    in_sem, out_sem, send_sem, recv_sem,
+    in_sem, send_sem, recv_sem,
 ):
     held = (held0, held1)
     me = lax.axis_index("ctx")
@@ -133,12 +122,12 @@
 
     devices = {
         (dx, dy, dk): (lax.rem(my_x + dx, 4) * 2 + lax.rem(my_y + dy, 2)) * 2 + lax.rem(my_k + dk, 2)
-        for dx, dy, dk in SLOTS
+        for dx, dy, dk in PLACES
     }
 
     barrier = pltpu.get_barrier_semaphore()
-    for send in OWN_SENDS:
-        pl.semaphore_signal(barrier, inc=1, device_id={"ctx": devices[send[3]]}, device_id_type=MESH)
+    for send in SENDS["own"]:
+        pl.semaphore_signal(barrier, inc=1, device_id={"ctx": devices[send[4]]}, device_id_type=MESH)
 
     loads = []
     for c in range(CONV):
@@ -157,11 +146,10 @@
         load.start()
 
     def copy_of(c, send):
-        source, part, parts, target, landing = send
-        where = pl.ds(part, parts)
+        source, slots, part, parts, target, landing = send
         return pltpu.make_async_remote_copy(
-            src_ref=held[c].at[SLOT_OF[source], where],
-            dst_ref=held[c].at[SLOT_OF[landing], where],
+            src_ref=held[c].at[pl.ds(source, slots), pl.ds(part, parts)],
+            dst_ref=held[c].at[pl.ds(landing, slots), pl.ds(part, parts)],
             send_sem=send_sem.at[c, SEND_INDEX[send]],
             recv_sem=recv_sem.at[c, SEND_INDEX[send]],
             device_id={"ctx": devices[target]},
@@ -180,11 +168,13 @@
             held[c][0, part, HALF : 2 * HALF, :] = jnp.where(low_half[c] == 0, second, first)
             held[c][0, part, 2 * HALF : CHUNK, :] = later[c]
 
-    def arrive(c, slot):
-        for send in ALL_SENDS:
-            if send[4] == slot:
+    def arrive(c, wave, shared):
+        for send in SENDS[wave]:
+            if (send[4] == BESIDE) == shared:
                 copy_of(c, send).wait_recv()
-        for send in FORWARDS.get(slot, ()):
+
+    def forward(c, wave):
+        for send in SENDS[wave]:
             copy_of(c, send).start()
 
     step_top[0] = jnp.full((GROUP * HALF, 128), FLOOR, jnp.float32)
@@ -208,7 +198,7 @@
     for h in range(FOLLOW_HEADS):
         f_query_mask[h * FOLLOW : (h + 1) * FOLLOW, :] = hidden
     for c in range(CONV):
-        for slot, offset in enumerate(SLOTS):
+        for slot, offset in enumerate(PLACES):
             owner = devices[offset]
             lower = jnp.minimum(order[c, 2 * owner], order[c, 2 * owner + 1])
             row, lane = iotas(HALF)
@@ -226,14 +216,13 @@
                 seen = (position >= last) & (lane == FOLLOW)
             f_mask[c, slot, 2 * HALF : CHUNK, :] = jnp.where(seen, 1.0, 0.0).astype(jnp.bfloat16)
 
-    pl.semaphore_wait(barrier, len(OWN_SENDS))
+    pl.semaphore_wait(barrier, len(SENDS["own"]))
     for c in range(CONV):
-        for send in OWN_SENDS:
-            copy_of(c, send).start()
+        forward(c, "own")
 
     def place(c, number):
         found = jnp.int32(0)
-        for slot, offset in enumerate(SLOTS):
+        for slot, offset in enumerate(PLACES):
             owner = devices[offset]
             lower = jnp.minimum(order[c, 2 * owner], order[c, 2 * owner + 1])
             found = jnp.where(lower == number, slot, found)
@@ -298,13 +287,6 @@
             )
         return units
 
-    stores = []
-
-    def store(src, dst):
-        copy = pltpu.make_async_copy(src, dst, out_sem.at[len(stores)])
-        copy.start()
-        stores.append(copy)
-
     def finish_follow(c):
         live = lax.broadcasted_iota(jnp.int32, (FOLLOW, HEAD_DIM), 0) + me * FOLLOW < lengths[c, 1]
         for h in range(GROUP):
@@ -313,8 +295,6 @@
             outf_ref[c, :, h * HEAD_DIM : (h + 1) * HEAD_DIM] = jnp.where(live, result, 0.0).astype(
                 jnp.bfloat16
             )
-        store(outf_ref.at[c], outf_hbm.at[c])
-
     def rest(c):
         mine = low_block[c]
         case = mine // 4
@@ -386,56 +366,55 @@
                     out_ref[c, half, :, h * HEAD_DIM : (h + 1) * HEAD_DIM] = jnp.where(
                         live, result, 0.0
                     ).astype(jnp.bfloat16)
-            columns = pl.ds(tile * PROMPT_HEADS * HEAD_DIM, PROMPT_HEADS * HEAD_DIM)
-            store(out_ref.at[c, :, :, columns], out_hbm.at[c, :, :, columns])
 
         finishes = [functools.partial(finish, tile) for tile in range(GROUP // PROMPT_HEADS)]
         return units, finishes
 
-    schedule(arrive, high_on_low, follow, finish_follow, rest, load_q, load_qf)
+    schedule(arrive, forward, high_on_low, follow, finish_follow, rest, load_q, load_qf)
     for c in range(CONV):
         for send in ALL_SENDS:
             copy_of(c, send).wait_send()
-    for copy in stores:
-        copy.wait()
-
-
-def schedule(arrive, high_on_low, follow, finish_follow, rest, load_q, load_qf):
-    near = (0, 1, 2, 3, 4, 5, 6, 7)
-    middle = (8, 9, 10, 11, 12, 13)
-    last = (14, 15)
+
+
+def schedule(arrive, forward, high_on_low, follow, finish_follow, rest, load_q, load_qf):
+    near = (0, 1, 2, 3, 8, 9, 10, 11)
+    middle = (4, 5, 6, 12, 13, 14)
+    last = (7, 15)
     far = middle + last
-
-    def wait_for(c, *slots):
+    following = {"own": "first", "first": "second", "second": "third"}
+
+    def chips(c, wave):
         def call():
-            for slot in slots:
-                arrive(c, slot)
+            arrive(c, wave, False)
+            forward(c, following[wave])
 
         return call
 
-    first = ((3, 0, 0), (1, 0, 0), (0, 1, 0))
-    first_shared = ((0, 0, 1), (3, 0, 1), (1, 0, 1), (0, 1, 1))
-    second = ((3, 1, 0), (1, 1, 0))
-    middle_shared = ((3, 1, 1), (1, 1, 1), (2, 0, 1))
+    def cores(c, *waves):
+        def call():
+            for wave in waves:
+                arrive(c, wave, True)
+
+        return call
+
     load_qf.wait()
     for load in load_q:
         load.wait()
     h, f = high_on_low(0, near, True), follow(0, near, True)
-    items = [wait_for(0, *first), wait_for(0, *first_shared)]
-    items += h[:2] + [wait_for(1, *first)] + h[2:] + f
+    items = [chips(0, "own"), cores(0, "own", "first")]
+    items += h + [chips(1, "own")] + f
     h, f = high_on_low(1, near, True), follow(1, near, True)
-    items += [wait_for(1, *first_shared), wait_for(0, (2, 0, 0))]
-    items += h[:3] + [wait_for(0, *second)] + h[3:] + [wait_for(1, (2, 0, 0))] + f
+    items += [cores(1, "own", "first")] + h + [chips(0, "first")] + f
     h, f = high_on_low(0, middle, False), follow(0, middle, False)
-    items += [wait_for(0, *middle_shared)]
-    items += h[:2] + [wait_for(1, *second)] + h[2:] + f[:1] + [wait_for(0, (2, 1, 0))] + f[1:]
+    items += [cores(0, "second")] + h + [chips(1, "first")] + f[:1] + [chips(0, "second")] + f[1:]
     h, f = high_on_low(0, last, False), follow(0, last, False)
-    items += [wait_for(0, (2, 1, 1))] + h + f + [wait_for(1, (2, 1, 0))]
+    items += [cores(0, "third")] + h + f
     units, finishes = rest(0)
-    items += units[:4] + [functools.partial(finish_follow, 0)] + units[4:10] + finishes[:1]
+    items += units[:2] + [chips(1, "second")] + units[2:4]
+    items += [functools.partial(finish_follow, 0)] + units[4:10] + finishes[:1]
     items += units[10:11] + finishes[1:2] + units[11:]
     h, f = high_on_low(1, far, False), follow(1, far, False)
-    items += [wait_for(1, *middle_shared, (2, 1, 1))]
+    items += [cores(1, "second", "third")]
     items += f[:1] + finishes[2:3] + f[1:] + finishes[3:] + h
     units, finishes = rest(1)
     items += units[:4] + [functools.partial(finish_follow, 1)] + units[4:10] + finishes[:1]
@@ -452,11 +431,11 @@
     out, out_follow = pl.pallas_call(
         kernel,
         out_shape=(
-            jax.ShapeDtypeStruct(halves + (width,), bf16),
-            jax.ShapeDtypeStruct((CONV, FOLLOW, width), bf16),
+            pltpu.VMEM(halves + (width,), bf16),
+            pltpu.VMEM((CONV, FOLLOW, width), bf16),
         ),
         in_specs=[smem, smem] + [any_space] * 6,
-        out_specs=(any_space, any_space),
+        out_specs=(pl.BlockSpec(memory_space=pltpu.VMEM),) * 2,
         scratch_shapes=[
             pltpu.VMEM(halves + (width,), bf16),
             pltpu.VMEM(halves + (HEAD_DIM,), bf16),
@@ -464,8 +443,6 @@
             pltpu.VMEM((CONV, FOLLOW, width), bf16),
             pltpu.VMEM((CONV, FOLLOW, HEAD_DIM), bf16),
             pltpu.VMEM((CONV, FOLLOW, HEAD_DIM), bf16),
-            pltpu.VMEM(halves + (width,), bf16),
-            pltpu.VMEM((CONV, FOLLOW, width), bf16),
             pltpu.VMEM((CTX, 2, CHUNK, HEAD_DIM), bf16),
             pltpu.VMEM((CTX, 2, CHUNK, HEAD_DIM), bf16),
             pltpu.VMEM((CONV, CTX, CHUNK, HEAD_DIM), bf16),
@@ -477,12 +454,11 @@
             pltpu.VMEM((CONV, GROUP * FOLLOW, HEAD_DIM), f32),
             pltpu.VMEM((CONV, GROUP * FOLLOW, 2 * HEAD_DIM), f32),
             pltpu.SemaphoreType.DMA((11,)),
-            pltpu.SemaphoreType.DMA((CONV + CONV * (GROUP // PROMPT_HEADS),)),
             pltpu.SemaphoreType.DMA((CONV, len(ALL_SENDS))),
             pltpu.SemaphoreType.DMA((CONV, len(ALL_SENDS))),
         ],
         compiler_params=pltpu.CompilerParams(
-            collective_id=0, has_side_effects=True, vmem_limit_bytes=63 << 20
+            collective_id=0, has_side_effects=True, vmem_limit_bytes=61 << 20
         ),
         cost_estimate=pl.CostEstimate(
             flops=7_400_000_000, bytes_accessed=8_000_000, transcendentals=15_000_000

time: 46.6 us -> 43.8 us (0.940)
  local copies, waits for them, and re-layouts: 3.48 us -> 1.85 us
  Pallas kernels: 42.3 us -> 41.2 us
    unnamed x4 -> x2, local copies, waits for them, and re-layouts: 3.48 us -> 1.85 us
    pallas_call x1, Pallas kernels: 42.3 us -> 41.2 us  [on_device(): pl.pallas_call(kernel, out_shape=(pltpu.VMEM(halves + (width,), bf16), pl...]
where the time goes in v3:
time: 43.8 us; the launch traced here: 43.7 us
  Pallas kernels  41.2 us (94%)
  local copies, waits for them, and re-layouts  1.85 us (4%)
  between operations  0.64 us (1%)
    pallas_call x1, Pallas kernels, on_device(): pl.pallas_call(kernel, out_shape=(pltpu.VMEM(halves + (width,), bf16), pl...  41.2 us
    unnamed x2, local copies, waits for them, and re-layouts  1.85 us

profile of v3, /device:TPU:1, one launch (start us, length us, event | category | flops | bytes accessed | tf_op | source)
XLA Modules:
  0.0 43.7 jit_solution(14908707797179519479)
XLA Ops:
  0.6 41.2 %shard_map.95 = (bf16[2,2,96,2048]{3,2,1,0:T(8,128)(2,1)S(1)}, bf16[2,32,2048]{2,1,0:T(8,128)(2,1)S(1)}) custom-call(s32[2,2]{1,0:T(2,128)} %lengths.1, s32[2,32]{1,0:T(2,128)} %order.1, bf16[2,2,96,2048]{3,2,1,0:T(8,128)(2,1)} %bitcast.5, bf16[2,2,96,128]{3,2,1,0:T(8,128)(2,1)} %bitcast.6, bf16[2,2,96,128]{3,2,1,0:T(8,128)(2,1)} %bitcast.7, ...), custom_call_target="tpu_custom_call" | custom-call | flops 7400000000 | bytes 8000000 | tf_op jit(solution)/shard_map/pallas_call | solution.py:431
  41.8 1.1 %copy.12 = bf16[2,192,2048]{2,1,0:T(8,128)(2,1)} copy(bf16[2,192,2048]{2,1,0:T(8,128)(2,1)S(1)} %bitcast.4) | data formatting | bytes 3145728
  43.0 0.7 %copy.13 = bf16[2,32,2048]{2,1,0:T(8,128)(2,1)} copy(bf16[2,32,2048]{2,1,0:T(8,128)(2,1)S(1)} %get-tuple-element.7) | data formatting | bytes 524288

commit v4 on v3

--- a/solution.py
+++ b/solution.py
@@ -177,6 +177,10 @@
         for send in SENDS[wave]:
             copy_of(c, send).start()
 
+    pl.semaphore_wait(barrier, len(SENDS["own"]))
+    for c in range(CONV):
+        forward(c, "own")
+
     step_top[0] = jnp.full((GROUP * HALF, 128), FLOOR, jnp.float32)
     step_total[0] = jnp.zeros((GROUP * HALF, 2 * HEAD_DIM), jnp.float32)
 
@@ -216,10 +220,6 @@
                 seen = (position >= last) & (lane == FOLLOW)
             f_mask[c, slot, 2 * HALF : CHUNK, :] = jnp.where(seen, 1.0, 0.0).astype(jnp.bfloat16)
 
-    pl.semaphore_wait(barrier, len(SENDS["own"]))
-    for c in range(CONV):
-        forward(c, "own")
-
     def place(c, number):
         found = jnp.int32(0)
         for slot, offset in enumerate(PLACES):
@@ -400,13 +400,12 @@
     load_qf.wait()
     for load in load_q:
         load.wait()
-    h, f = high_on_low(0, near, True), follow(0, near, True)
-    items = [chips(0, "own"), cores(0, "own", "first")]
-    items += h + [chips(1, "own")] + f
+    items = [chips(0, "own")] + follow(0, near[:4], True) + [cores(0, "own", "first")]
+    items += high_on_low(0, near, True) + [chips(1, "own")] + follow(0, near[4:], False)
     h, f = high_on_low(1, near, True), follow(1, near, True)
     items += [cores(1, "own", "first")] + h + [chips(0, "first")] + f
     h, f = high_on_low(0, middle, False), follow(0, middle, False)
-    items += [cores(0, "second")] + h + [chips(1, "first")] + f[:1] + [chips(0, "second")] + f[1:]
+    items += [cores(0, "second")] + h + f[:1] + [chips(1, "first"), chips(0, "second")] + f[1:]
     h, f = high_on_low(0, last, False), follow(0, last, False)
     items += [cores(0, "third")] + h + f
     units, finishes = rest(0)

time: 43.8 us -> 43.8 us (level)
  no operation moved by 1% of the time
where the time goes in v4:
time: 43.8 us; the launch traced here: 43.7 us
  Pallas kernels  41.2 us (94%)
  local copies, waits for them, and re-layouts  1.85 us (4%)
  between operations  0.64 us (1%)
    pallas_call x1, Pallas kernels, on_device(): pl.pallas_call(kernel, out_shape=(pltpu.VMEM(halves + (width,), bf16), pl...  41.2 us
    unnamed x2, local copies, waits for them, and re-layouts  1.85 us

profile of v4, /device:TPU:1, one launch (start us, length us, event | category | flops | bytes accessed | tf_op | source)
XLA Modules:
  0.0 43.7 jit_solution(10243747089370625676)
XLA Ops:
  0.6 41.2 %shard_map.95 = (bf16[2,2,96,2048]{3,2,1,0:T(8,128)(2,1)S(1)}, bf16[2,32,2048]{2,1,0:T(8,128)(2,1)S(1)}) custom-call(s32[2,2]{1,0:T(2,128)} %lengths.1, s32[2,32]{1,0:T(2,128)} %order.1, bf16[2,2,96,2048]{3,2,1,0:T(8,128)(2,1)} %bitcast.5, bf16[2,2,96,128]{3,2,1,0:T(8,128)(2,1)} %bitcast.6, bf16[2,2,96,128]{3,2,1,0:T(8,128)(2,1)} %bitcast.7, ...), custom_call_target="tpu_custom_call" | custom-call | flops 7400000000 | bytes 8000000 | tf_op jit(solution)/shard_map/pallas_call | solution.py:430
  41.9 1.1 %copy.12 = bf16[2,192,2048]{2,1,0:T(8,128)(2,1)} copy(bf16[2,192,2048]{2,1,0:T(8,128)(2,1)S(1)} %bitcast.4) | data formatting | bytes 3145728
  43.0 0.7 %copy.13 = bf16[2,32,2048]{2,1,0:T(8,128)(2,1)} copy(bf16[2,32,2048]{2,1,0:T(8,128)(2,1)S(1)} %get-tuple-element.7) | data formatting | bytes 524288
